TPU v7x, 32 devices: a whole 2x2x4 slice. The times are simulated.
32 devices in a mesh: ctx: 16 (over z, x, core), head: 2 (over y).
Axes of the slice: x: 2, y: 2, z: 4, core: 2. Of those that a mesh axis runs over, the one named last changes fastest.
Arguments:
- tokens: bfloat16 [4096, 768], P('ctx'), may hold values from -6 to 6
- w_qkv: bfloat16 [768, 3, 768], P('ctx', None, 'head'), may hold values from -0.3125 to 0.3125
- w_out: bfloat16 [768, 768], P('head', 'ctx'), may hold values from -1.25 to 1.25
- w_in: bfloat16 [768, 2, 1152], P('ctx', None, 'head'), may hold values from -0.21875 to 0.21875
- w_down: bfloat16 [1152, 768], P('head', 'ctx'), may hold values from -0.1875 to 0.1875
- gain_attn: bfloat16 [768], P('ctx'), may hold values from 0.099609375 to 1.8984375
- gain_mlp: bfloat16 [768], P('ctx'), may hold values from 0.099609375 to 1.8984375
- cotangent: bfloat16 [4096, 768], P('ctx'), may hold values from -6 to 6
Outputs:
- mixed: bfloat16 [4096, 768], P('ctx')
- grad_tokens: float32 [4096, 768], P('ctx')
- grad_qkv: float32 [768, 3, 768], P('ctx', None, 'head')
- grad_out: float32 [768, 768], P('head', 'ctx')
- grad_in: float32 [768, 2, 1152], P('ctx', None, 'head')
- grad_down: float32 [1152, 768], P('head', 'ctx')
- grad_gain_attn: float32 [768], P('ctx')
- grad_gain_mlp: float32 [768], P('ctx')
All inputs are finite; a program needn't handle non-finite values.
Results may differ from a plain program's by a relative error of at most 0.019.
The roundings to bfloat16 on the way count: a program that leaves them out, or rounds other values in their place, can miss the bound.
Values may be sent and summed in bfloat16 or wider, within the bound.
A program may use at most 192 MiB of HBM per device.

v0:
```python
import jax
import jax.numpy as jnp
from jax import lax
from jax.sharding import PartitionSpec as P

HEAD_DIM = 64


rope_base = 160000.0
epsilon = 1e-05
block_width = 512


def layer_norm(values, gain):
    centred = values - jnp.mean(values, axis=-1, keepdims=True)
    spread = jnp.mean(centred * centred, axis=-1, keepdims=True)
    return centred * lax.rsqrt(spread + epsilon) * gain


def rope_tables(first, rows):
    positions = (first + jnp.arange(rows, dtype=jnp.int32)).astype(jnp.float32)
    exponent = jnp.arange(HEAD_DIM // 2, dtype=jnp.int32).astype(jnp.float32) * (2.0 / HEAD_DIM)
    inverse = rope_base ** (-exponent)
    angles = positions[:, None] * inverse[None, :]
    angles = jnp.concatenate([angles, angles], axis=1)[:, None, :]
    return (jnp.cos(angles), jnp.sin(angles))


def turn_half(values):
    half = values.shape[-1] // 2
    return jnp.concatenate([-values[..., half:], values[..., :half]], axis=-1)


def rotate(values, cosine, sine):
    return values * cosine + turn_half(values) * sine


def unrotate(values, cosine, sine):
    return values * cosine - turn_half(values) * sine


def split_heads(flat_rows):
    return flat_rows.reshape(flat_rows.shape[0], -1, HEAD_DIM)


def in_blocks(block_step, state, pieces):
    rows_total = pieces[0].shape[0]
    stacked = tuple(
        (part.reshape((rows_total // block_width, block_width) + part.shape[1:]) for part in pieces)
    )

    def advance(carried, part):
        return (block_step(carried, part), None)

    state, _ = lax.scan(advance, state, stacked)
    return state


def shards(tokens, w_qkv, w_out, w_in, w_down, gain_attn, gain_mlp, cotangent):
    rows = tokens.shape[0]
    scale = HEAD_DIM ** (-0.5)
    full = (
        lax.all_gather(w_qkv, "ctx", axis=0, tiled=True),
        lax.all_gather(w_out, "ctx", axis=1, tiled=True),
        lax.all_gather(w_in, "ctx", axis=0, tiled=True),
        lax.all_gather(w_down, "ctx", axis=1, tiled=True),
        lax.all_gather(gain_attn, "ctx", axis=0, tiled=True),
        lax.all_gather(gain_mlp, "ctx", axis=0, tiled=True),
    )
    full_qkv, full_out, full_in, full_down, full_gain_attn, full_gain_mlp = full
    gain_first = full_gain_attn.astype(jnp.float32)
    gain_second = full_gain_mlp.astype(jnp.float32)
    width_here = full_qkv.shape[2]
    heads_here = width_here // HEAD_DIM
    cosine, sine = rope_tables(lax.axis_index("ctx") * rows, rows)
    inputs = tokens.astype(jnp.float32)
    normed = layer_norm(inputs, gain_first).astype(jnp.bfloat16)
    mixed_qkv = jnp.einsum("td,dcf->tcf", normed, full_qkv, preferred_element_type=jnp.float32)
    query_heads = rotate(split_heads(mixed_qkv[:, 0]), cosine, sine).astype(jnp.bfloat16)
    key_heads = rotate(split_heads(mixed_qkv[:, 1]), cosine, sine).astype(jnp.bfloat16)
    value_heads = split_heads(mixed_qkv[:, 2]).astype(jnp.bfloat16)
    key_rows = key_heads.reshape(rows, width_here)
    value_rows = value_heads.reshape(rows, width_here)

    def forward_block(state, pieces):
        peak, total, summed = state
        keys_piece = split_heads(pieces[0])
        values_piece = split_heads(pieces[1])
        scores = (
            jnp.einsum("the,phe->thp", query_heads, keys_piece, preferred_element_type=jnp.float32)
            * scale
        )
        top = jnp.maximum(peak, jnp.max(scores, axis=2))
        shrink = jnp.exp(peak - top)
        weights = jnp.exp(scores - top[:, :, None])
        total = total * shrink + jnp.sum(weights, axis=2)
        summed = summed * shrink[:, :, None] + jnp.einsum(
            "thp,phe->the",
            weights.astype(jnp.bfloat16),
            values_piece,
            preferred_element_type=jnp.float32,
        )
        return (top, total, summed)

    start_state = (
        jnp.full((rows, heads_here), -1e30, jnp.float32),
        jnp.zeros((rows, heads_here), jnp.float32),
        jnp.zeros((rows, heads_here, HEAD_DIM), jnp.float32),
    )
    peak, total, summed = in_blocks(
        forward_block,
        start_state,
        (
            lax.all_gather(key_rows, "ctx", axis=0, tiled=True),
            lax.all_gather(value_rows, "ctx", axis=0, tiled=True),
        ),
    )
    attended = summed / total[:, :, None]
    log_total = peak + jnp.log(total)
    attended_low = attended.reshape(rows, width_here).astype(jnp.bfloat16)
    branch = lax.psum(jnp.dot(attended_low, full_out, preferred_element_type=jnp.float32), "head")
    middle = inputs + branch
    normed_mlp = layer_norm(middle, gain_second).astype(jnp.bfloat16)
    gate_up = jnp.einsum("td,dcf->tcf", normed_mlp, full_in, preferred_element_type=jnp.float32)

    def activate(pair):
        return jax.nn.gelu(pair[:, 0], approximate=False) * pair[:, 1]

    hidden_values, activate_pull = jax.vjp(activate, gate_up)
    hidden = hidden_values.astype(jnp.bfloat16)
    branch_mlp = lax.psum(jnp.dot(hidden, full_down, preferred_element_type=jnp.float32), "head")
    mixed = (middle + branch_mlp).astype(jnp.bfloat16)
    back = (
        lax.all_gather(w_qkv, "ctx", axis=0, tiled=True),
        lax.all_gather(w_out, "ctx", axis=1, tiled=True),
        lax.all_gather(w_in, "ctx", axis=0, tiled=True),
        lax.all_gather(w_down, "ctx", axis=1, tiled=True),
        lax.all_gather(gain_attn, "ctx", axis=0, tiled=True),
        lax.all_gather(gain_mlp, "ctx", axis=0, tiled=True),
    )
    back_qkv, back_out, back_in, back_down, back_gain_attn, back_gain_mlp = back
    grad_output = cotangent.astype(jnp.float32)
    grad_down = jnp.einsum("tf,td->fd", hidden, cotangent, preferred_element_type=jnp.float32)
    grad_hidden = jnp.einsum("td,fd->tf", cotangent, back_down, preferred_element_type=jnp.float32)
    grad_pair = activate_pull(grad_hidden)[0].astype(jnp.bfloat16)
    grad_in = jnp.einsum("td,tcf->dcf", normed_mlp, grad_pair, preferred_element_type=jnp.float32)
    grad_normed_mlp = lax.psum(
        jnp.einsum("tcf,dcf->td", grad_pair, back_in, preferred_element_type=jnp.float32), "head"
    )
    _, second_pull = jax.vjp(layer_norm, middle, back_gain_mlp.astype(jnp.float32))
    grad_middle_norm, grad_gain_mlp = second_pull(grad_normed_mlp)
    grad_middle = grad_output + grad_middle_norm
    grad_attn = grad_middle.astype(jnp.bfloat16)
    grad_out = jnp.einsum("tf,td->fd", attended_low, grad_attn, preferred_element_type=jnp.float32)
    grad_rows = jnp.einsum(
        "td,fd->tf", grad_attn, back_out, preferred_element_type=jnp.float32
    ).astype(jnp.bfloat16)
    grad_heads = split_heads(grad_rows)
    correction = jnp.sum(grad_heads.astype(jnp.float32) * attended, axis=2)

    def query_block(grad_query, pieces):
        keys_piece = split_heads(pieces[0])
        values_piece = split_heads(pieces[1])
        scores = (
            jnp.einsum("the,phe->thp", query_heads, keys_piece, preferred_element_type=jnp.float32)
            * scale
        )
        probs = jnp.exp(scores - log_total[:, :, None])
        grad_probs = jnp.einsum(
            "the,phe->thp", grad_heads, values_piece, preferred_element_type=jnp.float32
        )
        grad_scores = (probs * (grad_probs - correction[:, :, None])).astype(jnp.bfloat16)
        return grad_query + scale * jnp.einsum(
            "thp,phe->the", grad_scores, keys_piece, preferred_element_type=jnp.float32
        )

    def key_block(state, pieces):
        grad_key, grad_value = state
        queries_piece = split_heads(pieces[0])
        grads_piece = split_heads(pieces[1])
        lse_piece = pieces[2]
        delta_piece = pieces[3]
        scores = (
            jnp.einsum("phe,the->pht", queries_piece, key_heads, preferred_element_type=jnp.float32)
            * scale
        )
        probs = jnp.exp(scores - lse_piece[:, :, None])
        grad_value = grad_value + jnp.einsum(
            "pht,phe->the",
            probs.astype(jnp.bfloat16),
            grads_piece,
            preferred_element_type=jnp.float32,
        )
        grad_probs = jnp.einsum(
            "phe,the->pht", grads_piece, value_heads, preferred_element_type=jnp.float32
        )
        grad_scores = (probs * (grad_probs - delta_piece[:, :, None])).astype(jnp.bfloat16)
        grad_key = grad_key + scale * jnp.einsum(
            "pht,phe->the", grad_scores, queries_piece, preferred_element_type=jnp.float32
        )
        return (grad_key, grad_value)

    zero_heads = jnp.zeros((rows, heads_here, HEAD_DIM), jnp.float32)
    query_wire = query_heads.reshape(rows, width_here)
    grad_query = in_blocks(
        query_block,
        zero_heads,
        (
            lax.all_gather(key_rows, "ctx", axis=0, tiled=True),
            lax.all_gather(value_rows, "ctx", axis=0, tiled=True),
        ),
    )
    grad_key, grad_value = in_blocks(
        key_block,
        (zero_heads, zero_heads),
        (
            lax.all_gather(query_wire.astype(jnp.float32), "ctx", axis=0, tiled=True).astype(
                jnp.bfloat16
            ),
            lax.all_gather(grad_rows.astype(jnp.float32), "ctx", axis=0, tiled=True).astype(
                jnp.bfloat16
            ),
            lax.all_gather(log_total, "ctx", axis=0, tiled=True),
            lax.all_gather(correction, "ctx", axis=0, tiled=True),
        ),
    )
    grad_query_plain = unrotate(grad_query, cosine, sine).reshape(rows, width_here)
    grad_key_plain = unrotate(grad_key, cosine, sine).reshape(rows, width_here)
    grad_triple = jnp.stack(
        [grad_query_plain, grad_key_plain, grad_value.reshape(rows, width_here)], axis=1
    ).astype(jnp.bfloat16)
    grad_qkv = jnp.einsum("td,tcf->dcf", normed, grad_triple, preferred_element_type=jnp.float32)
    grad_normed = lax.psum(
        jnp.einsum("tcf,dcf->td", grad_triple, back_qkv, preferred_element_type=jnp.float32), "head"
    )
    _, first_pull = jax.vjp(layer_norm, inputs, back_gain_attn.astype(jnp.float32))
    grad_input_norm, grad_gain_attn = first_pull(grad_normed)
    grad_tokens = grad_middle + grad_input_norm
    owned = (
        lax.psum_scatter(grad_qkv, "ctx", scatter_dimension=0, tiled=True),
        lax.psum_scatter(grad_out, "ctx", scatter_dimension=1, tiled=True),
        lax.psum_scatter(grad_in, "ctx", scatter_dimension=0, tiled=True),
        lax.psum_scatter(grad_down, "ctx", scatter_dimension=1, tiled=True),
        lax.psum_scatter(grad_gain_attn, "ctx", scatter_dimension=0, tiled=True),
        lax.psum_scatter(grad_gain_mlp, "ctx", scatter_dimension=0, tiled=True),
    )
    return (mixed, grad_tokens, owned[0], owned[1], owned[2], owned[3], owned[4], owned[5])


def solution(mesh):
    in_specs = (
        P("ctx", None),
        P("ctx", None, "head"),
        P("head", "ctx"),
        P("ctx", None, "head"),
        P("head", "ctx"),
        P("ctx"),
        P("ctx"),
        P("ctx", None),
    )
    out_specs = (
        P("ctx", None),
        P("ctx", None),
        P("ctx", None, "head"),
        P("head", "ctx"),
        P("ctx", None, "head"),
        P("head", "ctx"),
        P("ctx"),
        P("ctx"),
    )
    return jax.shard_map(shards, mesh=mesh, in_specs=in_specs, out_specs=out_specs, check_vma=False)
```

profile of v0, /device:TPU:0, one launch (start us, length us, event | category | flops | bytes accessed | tf_op | source)
XLA Modules:
  0.0 789.8 jit_solution(8632186800085806296)
XLA Ops:
  11.6 35.7 %all-reduce.8 = (bf16[768]{0:T(1024)(128)(2,1)S(1)}, bf16[768]{0:T(1024)(128)(2,1)}) all-reduce(bf16[768]{0:T(1024)(128)(2,1)S(1)} %dynamic-update-slice, bf16[768]{0:T(1024)(128)(2,1)S(1)} %dynamic-update-slice.1), channel_id=1, replica_groups=mesh['ctx'=16,'head'=2] {'ctx'}, use_global_device_ids=true, to_apply=%add.2 | all-reduce | flops 1536 | bytes 6144
  50.3 3.2 all-gather.8.cloned.1.call-done
  53.5 2.4 fusion.87
  59.4 23.1 %all_gather.48 = bf16[384,768]{0,1:T(8,128)(2,1)} all-gather(bf16[384,48]{0,1:T(8,128)(2,1)S(1)} %copy-done.37), channel_id=1, replica_groups=mesh['ctx'=16,'head'=2] {'ctx'}, dimensions={1}, use_global_device_ids=true | all-gather | bytes 626688 | tf_op jit(solution)/shard_map/all_gather | solution.py:64
  82.5 21.7 %all-gather.10.cloned.1.call-done = bf16[4096,384]{1,0:T(8,128)(2,1)} async-done(((bf16[256,384]{1,0:T(8,128)(2,1)}), bf16[4096,384]{1,0:T(8,128)(2,1)}) %all-gather.10.cloned.1.call-update) | async-done | bytes 3145744 | tf_op jit(solution)/shard_map/all_gather | solution.py:114
  104.2 4.6 copy.72
  108.8 41.7 %all-gather.18.cloned.1.call-done = bf16[4096,1,384]{2,0,1:T(8,128)(2,1)} async-done(((bf16[256,1,384]{2,0,1:T(8,128)(2,1)}), bf16[4096,1,384]{2,0,1:T(8,128)(2,1)}) %all-gather.18.cloned.1.call-update) | async-done | bytes 3145744 | tf_op jit(solution)/shard_map/all_gather | solution.py:115
  150.5 4.7 copy.73
  155.1 41.9 %while.39 = (s32[]{:T(128)}, f32[256,6]{0,1:T(8,128)S(1)}, f32[256,6]{0,1:T(8,128)}, f32[256,6,64]{0,2,1:T(8,128)}, bf16[8,512,384]{1,2,0:T(8,128)(2,1)}, /*inde...) while((s32[]{:T(128)}, f32[256,6]{0,1:T(8,128)S(1)}, ...), condition=%wide.region_5.6_spmd.clone, body=%wide.region_2.5_spmd.clone.sunk | while | flops 207920640 | bytes 16072925 | solution.py:55
  198.2 2.4 fusion.110
  202.4 22.0 %all_gather.51 = bf16[576,768]{0,1:T(8,128)(2,1)S(1)} all-gather(bf16[576,48]{0,1:T(8,128)(2,1)S(1)} %copy-done.34), channel_id=1, replica_groups=mesh['ctx'=16,'head'=2] {'ctx'}, dimensions={1}, use_global_device_ids=true | all-gather | bytes 940032 | tf_op jit(solution)/shard_map/all_gather | solution.py:66
  224.8 9.1 %all-reduce.13.cloned.1.call-done = f32[256,768]{1,0:T(8,128)} async-done(((f32[256,768]{1,0:T(8,128)}), f32[256,768]{1,0:T(8,128)}) %all-reduce.13.cloned.1.call-update) | async-done | bytes 786448 | tf_op jit(solution)/shard_map/psum | solution.py:121
  235.5 42.4 %all-gather.12.cloned.1.call-done = bf16[768,2,576]{2,0,1:T(8,128)(2,1)} async-done(((bf16[48,2,576]{2,0,1:T(8,128)(2,1)}), bf16[768,2,576]{2,0,1:T(8,128)(2,1)}) %all-gather.12.cloned.1.call-update) | async-done | bytes 1769488 | tf_op jit(solution)/shard_map/all_gather | solution.py:65
  277.9 2.5 fusion.100
  286.0 32.3 %all-reduce.15.cloned.1.call-done = f32[256,768]{1,0:T(8,128)} async-done(((f32[256,768]{1,0:T(8,128)}), f32[256,768]{1,0:T(8,128)}) %all-reduce.15.cloned.1.call-update) | async-done | bytes 786448 | tf_op jit(solution)/shard_map/psum | solution.py:147
  318.2 2.0 multiply_reduce_fusion
  322.8 2.3 convolution_convert_fusion
  326.9 23.2 %all_gather.53 = f32[4096,6]{0,1:T(8,128)} all-gather(f32[256,6]{0,1:T(8,128)S(1)} %log_add_fusion), channel_id=1, replica_groups=mesh['ctx'=16,'head'=2] {'ctx'}, dimensions={0}, use_global_device_ids=true | all-gather | bytes 104448 | tf_op jit(solution)/shard_map/all_gather | solution.py:223
  351.6 3.8 fusion.90
  358.1 19.3 %all_gather.55 = f32[4096,6]{0,1:T(8,128)} all-gather(f32[256,6]{0,1:T(8,128)S(1)} %multiply_reduce_fusion.3), channel_id=1, replica_groups=mesh['ctx'=16,'head'=2] {'ctx'}, dimensions={0}, use_global_device_ids=true | all-gather | bytes 104448 | tf_op jit(solution)/shard_map/all_gather | solution.py:224
  377.4 52.8 %while.40 = (s32[]{:T(128)}, f32[256,6,64]{0,2,1:T(8,128)}, bf16[8,512,384]{1,2,0:T(8,128)(2,1)}, bf16[256,6,64]{0,2,1:T(8,128)(2,1)}, f32[256,6]{0,1:T(8,128)S(...) while((s32[]{:T(128)}, f32[256,6,64]{0,2,1:T(8,128)}, ...), condition=%wide.region_15.16_spmd.clone, body=%wide.region_14.15_spmd.clone.sunk | while | flops 306216960 | bytes 10236019 | solution.py:55
  380.9 3.0 fusion.182
  383.8 1.9 constant_dynamic-slice_fusion.10
  387.3 3.1 fusion.182
  393.9 3.1 fusion.182
  400.5 3.1 fusion.182
  407.1 3.2 fusion.182
  410.3 1.9 constant_dynamic-slice_fusion.10
  413.8 3.1 fusion.182
  416.9 1.9 constant_dynamic-slice_fusion.10
  420.4 3.2 fusion.182
  423.6 1.9 constant_dynamic-slice_fusion.10
  427.1 3.2 fusion.182
  432.1 96.4 %while.41 = (s32[]{:T(128)}, f32[256,6,64]{0,2,1:T(8,128)}, f32[256,6,64]{0,2,1:T(8,128)}, bf16[8,512,384]{2,1,0:T(8,128)(2,1)}, bf16[256,6,64]{0,2,1:T(8,128)(2...) while((s32[]{:T(128)}, f32[256,6,64]{0,2,1:T(8,128)}, ...), condition=%wide.region_17.18_spmd.clone, body=%wide.region_16.17_spmd.clone.sunk | while | flops 409436160 | bytes 17780892 | solution.py:55
  432.1 2.0 constant_dynamic-slice_fusion.11
  438.5 3.2 fusion.191
  443.2 2.0 constant_dynamic-slice_fusion.11
  449.7 3.3 fusion.191
  453.0 2.5 fusion.192
  455.5 1.9 constant_dynamic-slice_fusion.11
  461.8 3.3 fusion.191
  465.2 2.5 fusion.192
  467.7 1.9 constant_dynamic-slice_fusion.11
  474.0 3.3 fusion.191
  477.4 2.5 fusion.192
  479.8 1.9 constant_dynamic-slice_fusion.11
  486.2 3.3 fusion.191
  489.6 2.5 fusion.192
  492.0 1.9 constant_dynamic-slice_fusion.11
  498.4 3.3 fusion.191
  501.7 2.5 fusion.192
  504.2 1.9 constant_dynamic-slice_fusion.11
  510.6 3.3 fusion.191
  513.9 2.5 fusion.192
  516.4 1.9 constant_dynamic-slice_fusion.11
  522.7 3.3 fusion.191
  526.1 2.5 fusion.192
  539.4 2.6 fusion.84
  544.6 40.5 %all-reduce.17.cloned.1.call-done = (f32[256,768]{1,0:T(8,128)}, f32[256,768]{1,0:T(8,128)}) async-done(((f32[256,768]{1,0:T(8,128)}, f32[256,768]{1,0:T(8,128)}), (f32[256,768]{1,0:T(8,128)}, f32[256,768]{1,0:T(8,128)})) %all-reduce.17.cloned.1.call-update) | async-done | bytes 1572880 | tf_op jit(solution)/shard_map/psum | solution.py:131
  588.2 33.8 %all-reduce.6 = (f32[768]{0:T(1024)S(1)}, f32[768]{0:T(1024)S(1)}) all-reduce(f32[768]{0:T(1024)S(1)} %get-tuple-element.322, f32[768]{0:T(1024)S(1)} %copy-done.40), channel_id=7, replica_groups=mesh['ctx'=16,'head'=2] {'ctx'}, use_global_device_ids=true, to_apply=%region_26.27.clone | all-reduce | flops 1536 | bytes 12288
  623.2 2.0 add_convert_fusion.1
  626.4 21.1 %reduce-scatter.7.cloned.1.call-done = f32[384,48]{0,1:T(8,128)} async-done(((f32[384,768]{0,1:T(8,128)}), f32[384,48]{0,1:T(8,128)}) %reduce-scatter.7.cloned.1.call-update) | async-done | bytes 73744 | tf_op jit(solution)/shard_map/reduce_scatter | solution.py:241
  647.5 64.3 %reduce-scatter.11.cloned.1.call-done = f32[576,48]{0,1:T(8,128)} async-done(((f32[576,768]{0,1:T(8,128)}), f32[576,48]{0,1:T(8,128)}) %reduce-scatter.11.cloned.1.call-update) | async-done | bytes 110608 | tf_op jit(solution)/shard_map/reduce_scatter | solution.py:243
  711.8 71.5 %reduce-scatter.5.cloned.1.call-done = f32[48,3,384]{2,0,1:T(8,128)} async-done(((f32[768,3,384]{2,0,1:T(8,128)}), f32[48,3,384]{2,0,1:T(8,128)}) %reduce-scatter.5.cloned.1.call-update) | async-done | bytes 221200 | tf_op jit(solution)/shard_map/reduce_scatter | solution.py:240
  (361 shorter events, 146.5 us)
Async XLA Ops:
  7.2 46.3 %all-gather.8.cloned.1.call-start = ((), (), s32[]{:S(2)}) async-start(), calls=%async_computation.4 | async-start | bytes 1880064 | tf_op jit(solution)/shard_map/all_gather | solution.py:63
  7.9 96.3 %all-gather.10.cloned.1.call-start = ((), (), s32[]{:S(2)}) async-start(), calls=%async_computation.5 | async-start | bytes 3342336 | tf_op jit(solution)/shard_map/all_gather | solution.py:114
  47.4 8.6 %copy-start.32 = (f32[768]{0:T(1024)}, f32[768]{0:T(1024)S(1)}, u32[]{:S(2)}) copy-start(f32[768]{0:T(1024)S(1)} %convert_element_type.106) | copy-start | bytes 9220
  47.6 8.8 %copy-start.25 = (f32[256,64]{0,1:T(8,128)}, f32[256,64]{0,1:T(8,128)S(1)}, u32[]{:S(2)}) copy-start(f32[256,64]{0,1:T(8,128)S(1)} %get-tuple-element.419) | copy-start | bytes 196612
  47.6 8.8 %copy-start.28 = (f32[256,64]{0,1:T(8,128)}, f32[256,64]{0,1:T(8,128)S(1)}, u32[]{:S(2)}) copy-start(f32[256,64]{0,1:T(8,128)S(1)} %get-tuple-element.418) | copy-start | bytes 196612
  49.0 7.0 copy-start.35
  50.2 5.8 copy-start.41
  50.2 5.7 copy-start.38
  56.4 3.0 copy-start.37
  58.5 92.0 %all-gather.18.cloned.1.call-start = ((), (), s32[]{:S(2)}) async-start(), calls=%async_computation.15 | async-start | bytes 3342336 | tf_op jit(solution)/shard_map/all_gather | solution.py:115
  59.3 174.6 %all-reduce.13.cloned.1.call-start = ((), (), s32[]{:S(2)}) async-start(), calls=%async_computation.6 | async-start | bytes 1572864 | tf_op jit(solution)/shard_map/psum | solution.py:121
  158.6 1.8 copy-start.30
  163.8 1.8 copy-start.30
  169.0 1.8 copy-start.30
  174.3 1.8 copy-start.30
  179.5 1.8 copy-start.30
  184.8 1.8 copy-start.30
  190.0 1.8 copy-start.30
  195.2 1.8 copy-start.30
  197.0 5.3 copy-start.45
  197.0 5.3 copy-start.34
  197.0 27.3 %copy-start.13 = (bf16[256,768]{1,0:T(8,128)(2,1)S(1)}, bf16[256,768]{1,0:T(8,128)(2,1)}, u32[]{:S(2)}) copy-start(bf16[256,768]{1,0:T(8,128)(2,1)} %param.21) | copy-start | bytes 1179652
  197.0 36.9 %copy-start.3 = (bf16[256,768]{1,0:T(8,128)(2,1)S(1)}, bf16[256,768]{1,0:T(8,128)(2,1)}, u32[]{:S(2)}) copy-start(bf16[256,768]{1,0:T(8,128)(2,1)} %param.14) | copy-start | bytes 1179652
  198.2 4.1 copy-start.21
  200.6 77.3 %all-gather.12.cloned.1.call-start = ((), (), s32[]{:S(2)}) async-start(), calls=%async_computation.7 | async-start | bytes 2088960 | tf_op jit(solution)/shard_map/all_gather | solution.py:65
  202.3 116.0 %all-reduce.15.cloned.1.call-start = ((), (), s32[]{:S(2)}) async-start(), calls=%async_computation.8 | async-start | bytes 1572864 | tf_op jit(solution)/shard_map/psum | solution.py:147
  224.8 55.6 %copy-start.16 = (f32[256,576]{0,1:T(8,128)}, f32[256,576]{0,1:T(8,128)S(1)}, u32[]{:S(2)}) copy-start(f32[256,576]{0,1:T(8,128)S(1)} %fusion.112) | copy-start | bytes 1769476
  235.2 116.4 %copy-start.1 = (f32[256,768]{1,0:T(8,128)}, f32[256,768]{1,0:T(8,128)S(1)}, u32[]{:S(2)}) copy-start(f32[256,768]{1,0:T(8,128)S(1)} %get-tuple-element.387) | copy-start | bytes 2359300
  280.4 2.9 copy-start.9
  283.3 66.8 %copy-start.19 = (bf16[256,576]{0,1:T(8,128)(2,1)}, bf16[256,576]{0,1:T(8,128)(2,1)S(1)}, u32[]{:S(2)}) copy-start(bf16[256,576]{0,1:T(8,128)(2,1)S(1)} %get-tuple-element.401) | copy-start | bytes 884740
  285.0 147.1 %all-gather.14.cloned.1.call-start = ((), (), s32[]{:S(2)}) async-start(), calls=%async_computation.9 | async-start | bytes 3342336 | tf_op jit(solution)/shard_map/all_gather | solution.py:217
  285.8 146.3 %all-gather.16.cloned.1.call-start = ((), (), s32[]{:S(2)}) async-start(), calls=%async_computation.10 | async-start | bytes 3342336 | tf_op jit(solution)/shard_map/all_gather | solution.py:220
  320.3 6.6 copy-start.31
  321.8 33.6 %copy-start.43 = (f32[256]{0:T(256)}, f32[256]{0:T(256)S(1)}, u32[]{:S(2)}) copy-start(f32[256]{0:T(256)S(1)} %negate_multiply_fusion.2) | copy-start | bytes 3076
  322.8 32.6 %copy-start.17 = (bf16[256,768]{1,0:T(8,128)(2,1)}, bf16[256,768]{1,0:T(8,128)(2,1)S(1)}, u32[]{:S(2)}) copy-start(bf16[256,768]{1,0:T(8,128)(2,1)S(1)} %fusion.73) | copy-start | bytes 1179652
  325.1 217.7 %reduce-scatter.9.cloned.1.call-start = ((), (), s32[]{:S(2)}) async-start(), calls=%async_computation.13 | async-start | bytes 4177920 | tf_op jit(solution)/shard_map/reduce_scatter | solution.py:242
  355.4 1.7 copy-start.7
  355.4 229.7 %all-reduce.17.cloned.1.call-start = ((), (), s32[]{:S(2)}) async-start(), calls=%async_computation.16 | async-start | bytes 3145728 | tf_op jit(solution)/shard_map/psum | solution.py:131
  434.3 1.7 copy-start
  445.4 1.7 copy-start
  457.6 1.7 copy-start
  469.8 1.7 copy-start
  482.0 1.7 copy-start
  494.2 1.7 copy-start
  506.3 1.7 copy-start
  518.5 1.7 copy-start
  528.5 3.1 copy-start.8
  528.5 5.6 copy-start.24
  531.6 4.2 copy-start.18
  531.6 4.2 copy-start.22
  535.8 111.7 %reduce-scatter.7.cloned.1.call-start = ((), (), s32[]{:S(2)}) async-start(), calls=%async_computation.12 | async-start | bytes 1253376 | tf_op jit(solution)/shard_map/reduce_scatter | solution.py:241
  537.3 2.1 copy-start.4
  537.3 2.1 copy-start.27
  537.3 2.1 copy-start.33
  537.3 2.1 copy-start.36
  537.3 2.1 copy-start.39
  537.3 174.4 %reduce-scatter.11.cloned.1.call-start = ((), (), s32[]{:S(2)}) async-start(), calls=%async_computation.14 | async-start | bytes 2088960 | tf_op jit(solution)/shard_map/reduce_scatter | solution.py:243
  539.3 244.0 %reduce-scatter.5.cloned.1.call-start = ((), (), s32[]{:S(2)}) async-start(), calls=%async_computation.11 | async-start | bytes 3760128 | tf_op jit(solution)/shard_map/reduce_scatter | solution.py:240
  542.0 44.6 %copy-start.42 = (f32[256]{0:T(256)S(1)}, f32[256]{0:T(256)}, u32[]{:S(2)}) copy-start(f32[256]{0:T(256)} %copy-done.41) | copy-start | bytes 3076
  542.0 46.2 %copy-start.40 = (f32[768]{0:T(1024)S(1)}, f32[768]{0:T(1024)}, u32[]{:S(2)}) copy-start(f32[768]{0:T(1024)} %get-tuple-element.320) | copy-start | bytes 9220
  542.0 81.2 %copy-start.2 = (f32[256,768]{1,0:T(8,128)S(1)}, f32[256,768]{1,0:T(8,128)}, u32[]{:S(2)}) copy-start(f32[256,768]{1,0:T(8,128)} %copy-done.1) | copy-start | bytes 2359300
  542.0 83.1 %copy-start.12 = (f32[256,768]{1,0:T(8,128)S(1)}, f32[256,768]{1,0:T(8,128)}, u32[]{:S(2)}) copy-start(f32[256,768]{1,0:T(8,128)} %copy-done.11) | copy-start | bytes 2359300
  542.0 83.1 %copy-start.44 = (f32[256]{0:T(256)S(1)}, f32[256]{0:T(256)}, u32[]{:S(2)}) copy-start(f32[256]{0:T(256)} %copy-done.43) | copy-start | bytes 3076
  585.1 40.0 %copy-start.10 = (f32[256,768]{1,0:T(8,128)S(1)}, f32[256,768]{1,0:T(8,128)}, u32[]{:S(2)}) copy-start(f32[256,768]{1,0:T(8,128)} %get-tuple-element.375) | copy-start | bytes 2359300
  (30 other events, 26.9 us)
Sparse Core Ops, SparseCore 0:
  10.3 43.1 all-gather.7
  58.6 45.4 all-gather.9
  106.4 43.9 all-gather.17
  200.7 33.1 all-reduce.12
  236.8 41.0 all-gather.11
  285.1 33.0 all-reduce.14
  320.5 46.1 all-gather.13
  369.0 43.7 all-gather.15
  416.6 69.3 reduce-scatter.8
  535.9 49.1 all-reduce.16
  589.3 58.0 reduce-scatter.6
  651.6 60.0 reduce-scatter.10
  716.2 67.0 reduce-scatter.4
where the time goes:
time: 794 us; the launch traced here: 790 us
  waiting for transfers between devices  349 us (44%)
  blocking collectives  157 us (20%)
  matrix products  139 us (18%)
  local copies, waits for them, and re-layouts  96.4 us (12%)
  other arithmetic  30.4 us (4%)
  between operations  16 us (2%)
    reduce_scatter x1, waiting for transfers between devices, shards(): lax.psum_scatter(grad_qkv, 'ctx', scatter_dimension=0, tiled=True)  71.5 us
    unnamed x2, blocking collectives  69.5 us
    reduce_scatter x1, waiting for transfers between devices, shards(): lax.psum_scatter(grad_down, 'ctx', scatter_dimension=1, tiled=True)  64.3 us
    dynamic_slice x40, local copies, waits for them, and re-layouts, in_blocks(): state, _ = lax.scan(advance, state, stacked)  51.2 us
    all_gather x1, waiting for transfers between devices, shards(): lax.all_gather(w_in, 'ctx', axis=0, tiled=True)  42.4 us
    all_gather x1, waiting for transfers between devices, shards(): lax.all_gather(value_rows, 'ctx', axis=0, tiled=True)  41.7 us
    psum x1, waiting for transfers between devices, shards(): lax.psum(jnp.dot(hidden, full_down, preferred_element_type=jnp.float32),...  40.5 us
    psum x1, waiting for transfers between devices, shards(): lax.psum(jnp.einsum('tcf,dcf->td', grad_pair, back_in, preferred_element_...  32.3 us
  transfers between devices with their start and end apart: 13, of which 10 were waited for; matrix products, arithmetic and copies ran while one was open for 26% of the time, Pallas kernels for 0%

commit v1 on v0

v1 whole, which is shorter than its diff:
```python
import functools

import jax
import jax.numpy as jnp
from jax import lax
from jax.experimental import pallas as pl
from jax.experimental.pallas import tpu as pltpu
from jax.sharding import PartitionSpec as P

HEAD_DIM = 64
PAIR = 2 * HEAD_DIM
MESH = pl.DeviceIdType.MESH
VMEM_LIMIT = 56 * 1024 * 1024
RESIDENT_LIMIT = 32 * 1024 * 1024

rope_base = 160000.0
epsilon = 1e-05
f32 = jnp.float32
bf16 = jnp.bfloat16


def layer_norm(values, gain):
    centred = values - jnp.mean(values, axis=-1, keepdims=True)
    spread = jnp.mean(centred * centred, axis=-1, keepdims=True)
    return centred * lax.rsqrt(spread + epsilon) * gain


def rope_tables(first, rows):
    positions = (first + jnp.arange(rows, dtype=jnp.int32)).astype(f32)
    exponent = jnp.arange(HEAD_DIM // 2, dtype=jnp.int32).astype(f32) * (2.0 / HEAD_DIM)
    inverse = rope_base ** (-exponent)
    angles = positions[:, None] * inverse[None, :]
    angles = jnp.concatenate([angles, angles], axis=1)[:, None, :]
    return (jnp.cos(angles), jnp.sin(angles))


def turn_half(values):
    half = values.shape[-1] // 2
    return jnp.concatenate([-values[..., half:], values[..., :half]], axis=-1)


def rotate(values, cosine, sine):
    return values * cosine + turn_half(values) * sine


def unrotate(values, cosine, sine):
    return values * cosine - turn_half(values) * sine


def split_heads(flat_rows):
    return flat_rows.reshape(flat_rows.shape[0], -1, HEAD_DIM)


class Ring:
    def __init__(self, devices):
        self.chips = devices // 2
        self.rights = self.chips // 2
        self.lefts = self.chips - 1 - self.rights
        self.me = lax.axis_index("ctx")
        self.head = lax.axis_index("head")
        chip = lax.div(self.me, 2)
        self.core = lax.rem(self.me, 2)
        side = lax.rem(chip, 2)
        level = lax.div(chip, 2)
        self.place = level + side * (self.chips - 1 - 2 * level)

    def chip_at(self, place):
        place = lax.rem(place + 2 * self.chips, self.chips)
        far = lax.div(place, self.chips // 2)
        return (1 - far) * 2 * place + far * (2 * (self.chips - 1 - place) + 1)

    def index(self, offset, core):
        return self.chip_at(self.place + offset) * 2 + core

    def neighbours(self):
        return (self.index(1, self.core), self.index(-1, self.core), self.me + 1 - 2 * self.core)

    def barrier(self):
        sem = pltpu.get_barrier_semaphore()
        for other in self.neighbours():
            pl.semaphore_signal(sem, inc=1, device_id=(other, self.head), device_id_type=MESH)
        pl.semaphore_wait(sem, 3)


class Gather:
    def __init__(self, ring, own, full, send, recv, local):
        self.ring, self.own, self.full = ring, own, full
        self.send, self.recv, self.local = send, recv, local
        self.right, self.left, self.sibling = ring.neighbours()

    def copies(self, kind, number, slot, target, first=False):
        return [
            pltpu.make_async_remote_copy(
                src_ref=own if first else full.at[slot],
                dst_ref=full.at[slot],
                send_sem=self.send.at[a, kind, number],
                recv_sem=self.recv.at[a, kind, number],
                device_id=(target, self.ring.head),
                device_id_type=MESH,
            )
            for a, (own, full) in enumerate(zip(self.own, self.full))
        ]

    def start(self, *where, first=False):
        for copy in self.copies(*where, first=first):
            copy.start()

    def arrive(self, kind, number, slot):
        for copy in self.copies(kind, number, slot, self.sibling):
            copy.wait_recv()

    def begin(self):
        ring = self.ring
        self.start(0, 0, ring.me, self.right, first=True)
        self.start(1, 0, ring.me, self.left, first=True)
        self.start(2, 0, ring.me, self.sibling, first=True)
        for a, (own, full) in enumerate(zip(self.own, self.full)):
            copy = pltpu.make_async_copy(own, full.at[ring.me], self.local.at[a])
            copy.start()
            copy.wait()

    def step(self, s):
        ring = self.ring
        slot = ring.index(-s, ring.core)
        self.arrive(0, s - 1, slot)

        @pl.when(s < ring.rights)
        def _():
            self.start(0, s, slot, self.right)

        self.start(2, s, slot, self.sibling)

        @pl.when(s <= ring.lefts)
        def _():
            other = ring.index(s, ring.core)
            self.arrive(1, s - 1, other)

            @pl.when(s < ring.lefts)
            def _():
                self.start(1, s, other, self.left)

            self.start(2, ring.rights + s, other, self.sibling)

    def sibling_step(self, s):
        ring = self.ring
        self.arrive(2, s, ring.index(-s, 1 - ring.core))

        @pl.when(s <= ring.lefts)
        def _():
            self.arrive(2, ring.rights + s, ring.index(s, 1 - ring.core))

    def sibling_first(self):
        self.arrive(2, 0, self.sibling)

    def finish(self):
        ring = self.ring

        def sent(kind):
            def one(number, carry):
                for copy in self.copies(kind, number, ring.me, self.sibling):
                    copy.wait_send()
                return carry

            return one

        lax.fori_loop(0, ring.rights, sent(0), 0)
        lax.fori_loop(0, ring.lefts, sent(1), 0)
        lax.fori_loop(0, ring.chips, sent(2), 0)


def gather_sems(arrays, devices):
    chips = devices // 2
    return [
        pltpu.SemaphoreType.DMA((arrays, 3, chips)),
        pltpu.SemaphoreType.DMA((arrays, 3, chips)),
        pltpu.SemaphoreType.DMA((arrays,)),
    ]


def params(number):
    return pltpu.CompilerParams(
        collective_id=number, has_side_effects=True, vmem_limit_bytes=VMEM_LIMIT
    )


whole_vmem = pl.BlockSpec(memory_space=pltpu.VMEM)
whole_any = pl.BlockSpec(memory_space=pl.ANY)


def gather_kernel(devices, own, full, send, recv, local):
    ring = Ring(devices)
    ring.barrier()
    gather = Gather(ring, [own], [full], send, recv, local)
    gather.begin()
    gather.sibling_first()

    def step(s, carry):
        gather.step(s)
        return carry

    lax.fori_loop(1, ring.rights + 1, step, 0)

    def late(s, carry):
        gather.sibling_step(s)
        return carry

    lax.fori_loop(1, ring.rights + 1, late, 0)
    gather.finish()


def all_gather(own, devices, number):
    return pl.pallas_call(
        functools.partial(gather_kernel, devices),
        out_shape=jax.ShapeDtypeStruct((devices,) + own.shape, own.dtype),
        in_specs=[whole_any],
        out_specs=whole_any,
        scratch_shapes=gather_sems(1, devices),
        compiler_params=params(number),
    )(own)


def nt(a, b):
    return lax.dot_general(a, b, (((1,), (1,)), ((), ())), preferred_element_type=f32)


def nn(a, b):
    return jnp.dot(a, b, preferred_element_type=f32)


def lane_mask(rows, side):
    lanes = lax.broadcasted_iota(jnp.int32, (rows, PAIR), 1)
    return (lanes >= HEAD_DIM) if side else (lanes < HEAD_DIM)


def masked_heads(source, offset, heads, target):
    for h in range(heads):
        start = offset + (h // 2) * PAIR
        block = source[:, start : start + PAIR].astype(f32)
        keep = lane_mask(block.shape[0], h % 2)
        target[h] = jnp.where(keep, block, 0.0).astype(bf16)


def visit(ring, gather, process):
    gather.begin()
    process(ring.me)
    gather.sibling_first()
    process(gather.sibling)

    def step(s, carry):
        gather.step(s)

        def half(other, carry):
            @pl.when(other == 1)
            def _():
                gather.sibling_step(s)

            core = ring.core + other * (1 - 2 * ring.core)
            ways = jnp.where(s <= ring.lefts, 2, 1)

            def way(w, carry):
                process(ring.index((2 * w - 1) * s, core))
                return carry

            return lax.fori_loop(0, ways, way, carry)

        return lax.fori_loop(0, 2, half, carry)

    lax.fori_loop(1, ring.rights + 1, step, 0)
    gather.finish()


def forward_kernel(devices, heads, q, kv, full, att, lse, qm, top, total, acc, send, recv, local, *stage):
    width = heads * HEAD_DIM
    ring = Ring(devices)
    ring.barrier()
    gather = Gather(ring, [kv], [full], send, recv, local)
    masked_heads(q, 0, heads, qm)
    top[...] = jnp.full_like(top, -1e30)
    total[...] = jnp.zeros_like(total)
    acc[...] = jnp.zeros_like(acc)

    def process(slot):
        block = full.at[slot]
        if stage:
            copy = pltpu.make_async_copy(block, stage[0], stage[1])
            copy.start()
            copy.wait()
            block = stage[0]
        for p in range(heads // 2):
            keys = block[:, p * PAIR : (p + 1) * PAIR]
            values = block[:, width + p * PAIR : width + (p + 1) * PAIR].T
            for side in range(2):
                h = 2 * p + side
                scores = nt(keys, qm[h])
                before = top[h : h + 1]
                peak = jnp.maximum(before, jnp.max(scores, axis=0, keepdims=True))
                shrink = jnp.exp(before - peak)
                weights = jnp.exp(scores - peak)
                top[h : h + 1] = peak
                total[h : h + 1] = total[h : h + 1] * shrink + jnp.sum(
                    weights, axis=0, keepdims=True
                )
                part = nn(values[side * HEAD_DIM : (side + 1) * HEAD_DIM], weights.astype(bf16))
                rows = slice(h * HEAD_DIM, (h + 1) * HEAD_DIM)
                acc[rows] = acc[rows] * shrink + part

    visit(ring, gather, process)
    for h in range(heads):
        rows = slice(h * HEAD_DIM, (h + 1) * HEAD_DIM)
        acc[rows] = acc[rows] / total[h : h + 1]
    att[...] = acc[...].T
    lse[...] = top[...] + jnp.log(jnp.maximum(total[...], 1e-37))


def resident(devices, rows, width):
    return devices * rows * width * 2 * 2 <= RESIDENT_LIMIT


def forward_attention(q, kv, devices, number):
    rows, width = q.shape
    heads = width // HEAD_DIM
    near = resident(devices, rows, 2 * width)
    return pl.pallas_call(
        functools.partial(forward_kernel, devices, heads),
        out_shape=(
            jax.ShapeDtypeStruct((devices,) + kv.shape, bf16),
            jax.ShapeDtypeStruct((rows, width), f32),
            jax.ShapeDtypeStruct((8, rows), f32),
        ),
        in_specs=[whole_vmem, whole_vmem if near else whole_any],
        out_specs=(whole_vmem if near else whole_any, whole_vmem, whole_vmem),
        scratch_shapes=[
            pltpu.VMEM((heads, rows, PAIR), bf16),
            pltpu.VMEM((8, rows), f32),
            pltpu.VMEM((8, rows), f32),
            pltpu.VMEM((width, rows), f32),
        ]
        + gather_sems(1, devices)
        + ([] if near else [pltpu.VMEM(kv.shape, bf16), pltpu.SemaphoreType.DMA]),
        compiler_params=params(number),
    )(q, kv)


def backward_kernel(
    devices, heads, qg, stats, kv, kv_all, dq, dk, dv, *rest
):
    full, stats_all = rest[:2]
    rest = rest[2:]
    qm, gm, km, vm, dqt, dka, dva, send, recv, local = rest[:10]
    stage = rest[10:]
    width = heads * HEAD_DIM
    ring = Ring(devices)
    ring.barrier()
    gather = Gather(ring, [qg, stats], [full, stats_all], send, recv, local)
    own = qg
    if stage:
        copies = [
            pltpu.make_async_copy(qg, stage[0], stage[3].at[0]),
            pltpu.make_async_copy(stats, stage[4], stage[3].at[1]),
        ]
        for copy in copies:
            copy.start()
        for copy in copies:
            copy.wait()
        own = stage[0]
    mine = stage[4] if stage else stats
    masked_heads(own, 0, heads, qm)
    masked_heads(own, width, heads, gm)
    masked_heads(kv, 0, heads, km)
    masked_heads(kv, width, heads, vm)
    dqt[...] = jnp.zeros_like(dqt)
    dka[...] = jnp.zeros_like(dka)
    dva[...] = jnp.zeros_like(dva)

    def process(slot):
        block, keyed, rows_of = full.at[slot], kv_all.at[slot], stats_all.at[slot]
        if stage:
            copies = [
                pltpu.make_async_copy(block, stage[0], stage[3].at[0]),
                pltpu.make_async_copy(keyed, stage[1], stage[3].at[1]),
                pltpu.make_async_copy(rows_of, stage[2], stage[3].at[2]),
            ]
            for copy in copies:
                copy.start()
            for copy in copies:
                copy.wait()
            block, keyed, rows_of = stage[:3]
        for p in range(heads // 2):
            first = slice(p * PAIR, (p + 1) * PAIR)
            second = slice(width + p * PAIR, width + (p + 1) * PAIR)
            keys = keyed[:, first]
            values = keyed[:, second]
            turned = keys.T
            queries = block[:, first]
            grads = block[:, second]
            for side in range(2):
                h = 2 * p + side
                probs = jnp.exp(nt(keys, qm[h]) - mine[h : h + 1])
                slope = nt(values, gm[h])
                small = (probs * (slope - mine[8 + h : 9 + h])).astype(bf16)
                rows = slice(h * HEAD_DIM, (h + 1) * HEAD_DIM)
                dqt[rows] += nn(turned[side * HEAD_DIM : (side + 1) * HEAD_DIM], small)
                probs = jnp.exp(nt(km[h], queries) - rows_of[h : h + 1])
                slope = nt(vm[h], grads)
                small = (probs * (slope - rows_of[8 + h : 9 + h])).astype(bf16)
                dva[h] += nn(probs.astype(bf16), grads)
                dka[h] += nn(small, queries)

    visit(ring, gather, process)
    dq[...] = dqt[...].T * (HEAD_DIM ** (-0.5))
    keep = lane_mask(dk.shape[0], 0)
    for p in range(heads // 2):
        first = slice(p * PAIR, (p + 1) * PAIR)
        dk[:, first] = jnp.where(keep, dka[2 * p], dka[2 * p + 1])
        dv[:, first] = jnp.where(keep, dva[2 * p], dva[2 * p + 1])


def backward_attention(qg, stats, kv, kv_all, devices, number):
    rows = qg.shape[0]
    width = qg.shape[1] // 2
    heads = width // HEAD_DIM
    near = resident(devices, rows, 2 * width)
    flat = jax.ShapeDtypeStruct((rows, width), f32)
    out_shape = [flat, flat, flat]
    out_specs = [whole_vmem] * 3
    buffers = []
    if near:
        buffers = [
            pltpu.VMEM((devices,) + qg.shape, bf16),
            pltpu.VMEM((devices,) + stats.shape, f32),
        ]
    else:
        out_shape += [
            jax.ShapeDtypeStruct((devices,) + qg.shape, bf16),
            jax.ShapeDtypeStruct((devices,) + stats.shape, f32),
        ]
        out_specs += [whole_any] * 2
    space = whole_vmem if near else whole_any
    return pl.pallas_call(
        functools.partial(backward_kernel, devices, heads),
        out_shape=tuple(out_shape),
        in_specs=[space, space, whole_vmem, space],
        out_specs=tuple(out_specs),
        scratch_shapes=buffers
        + [
            pltpu.VMEM((heads, rows, PAIR), bf16),
            pltpu.VMEM((heads, rows, PAIR), bf16),
            pltpu.VMEM((heads, rows, PAIR), bf16),
            pltpu.VMEM((heads, rows, PAIR), bf16),
            pltpu.VMEM((width, rows), f32),
            pltpu.VMEM((heads, rows, PAIR), f32),
            pltpu.VMEM((heads, rows, PAIR), f32),
        ]
        + gather_sems(2, devices)
        + (
            []
            if near
            else [
                pltpu.VMEM(qg.shape, bf16),
                pltpu.VMEM(kv.shape, bf16),
                pltpu.VMEM(stats.shape, f32),
                pltpu.SemaphoreType.DMA((3,)),
                pltpu.VMEM(stats.shape, f32),
            ]
        ),
        compiler_params=params(number),
    )(qg, stats, kv, kv_all)[:3]


def exchange_kernel(own, out, arrived, send, recv):
    other = 1 - lax.axis_index("head")
    here = lax.axis_index("ctx")
    sem = pltpu.get_barrier_semaphore()
    pl.semaphore_signal(sem, inc=1, device_id=(here, other), device_id_type=MESH)
    pl.semaphore_wait(sem, 1)
    copy = pltpu.make_async_remote_copy(
        src_ref=own, dst_ref=arrived, send_sem=send, recv_sem=recv,
        device_id=(here, other), device_id_type=MESH,
    )
    copy.start()
    copy.wait()
    out[...] = own[...].astype(f32) + arrived[...].astype(f32)


def head_sum(part, number):
    part = part.astype(bf16)
    return pl.pallas_call(
        exchange_kernel,
        out_shape=jax.ShapeDtypeStruct(part.shape, f32),
        in_specs=[whole_vmem],
        out_specs=whole_vmem,
        scratch_shapes=[
            pltpu.VMEM(part.shape, bf16), pltpu.SemaphoreType.DMA, pltpu.SemaphoreType.DMA,
        ],
        compiler_params=params(number),
    )(part)


def scatter_kernel(devices, part, out, stage, rights, lefts, send, recv):
    ring = Ring(devices)
    right, left, sibling = ring.neighbours()
    ring.barrier()

    def make(source, target, kind, number, device):
        return pltpu.make_async_remote_copy(
            src_ref=source, dst_ref=target,
            send_sem=send.at[kind, number], recv_sem=recv.at[kind, number],
            device_id=(device, ring.head), device_id_type=MESH,
        )

    def launch_chip(step, carry):
        chip = ring.chip_at(ring.place + ring.rights - step)
        make(part.at[chip * 2 + 1 - ring.core], stage.at[chip], 2, chip, sibling).start()
        return carry

    lax.fori_loop(0, ring.chips, launch_chip, 0)

    def landed(step, carry):
        chip = ring.chip_at(ring.place + ring.rights - step)
        make(part.at[chip * 2 + 1 - ring.core], stage.at[chip], 2, chip, sibling).wait()
        stage[chip] = (
            stage[chip].astype(f32) + part[chip * 2 + ring.core].astype(f32)
        ).astype(bf16)
        return carry

    lax.fori_loop(0, ring.chips, landed, 0)
    make(stage.at[ring.chip_at(ring.place + ring.rights)], rights.at[0], 0, 0, right).start()
    make(stage.at[ring.chip_at(ring.place - ring.lefts)], lefts.at[0], 1, 0, left).start()

    def step(s, carry):
        make(rights.at[s - 1], rights.at[s - 1], 0, s - 1, right).wait_recv()
        chip = ring.chip_at(ring.place + ring.rights - s)
        rights[s - 1] = (rights[s - 1].astype(f32) + stage[chip].astype(f32)).astype(bf16)
        make(rights.at[s - 1], rights.at[s], 0, s, right).start()

        @pl.when(s < ring.lefts)
        def _():
            make(lefts.at[s - 1], lefts.at[s - 1], 1, s - 1, left).wait_recv()
            chip = ring.chip_at(ring.place - ring.lefts + s)
            lefts[s - 1] = (lefts[s - 1].astype(f32) + stage[chip].astype(f32)).astype(bf16)
            make(lefts.at[s - 1], lefts.at[s], 1, s, left).start()

        return carry

    lax.fori_loop(1, ring.rights, step, 0)
    make(lefts.at[ring.lefts - 1], lefts.at[ring.lefts - 1], 1, ring.lefts - 1, left).wait_recv()
    make(rights.at[ring.rights - 1], rights.at[ring.rights - 1], 0, ring.rights - 1, right).wait_recv()
    out[...] = (
        stage[ring.chip_at(ring.place)].astype(f32)
        + rights[ring.rights - 1].astype(f32)
        + lefts[ring.lefts - 1].astype(f32)
    )

    def sent(kind):
        def one(number, carry):
            make(stage.at[0], stage.at[0], kind, number, right).wait_send()
            return carry

        return one

    lax.fori_loop(0, ring.rights, sent(0), 0)
    lax.fori_loop(0, ring.lefts, sent(1), 0)


def reduce_scatter(part, devices, number):
    block = part.shape[1:]
    chips = devices // 2
    return pl.pallas_call(
        functools.partial(scatter_kernel, devices),
        out_shape=jax.ShapeDtypeStruct(block, f32),
        in_specs=[whole_vmem],
        out_specs=whole_vmem,
        scratch_shapes=[
            pltpu.VMEM((chips,) + block, bf16),
            pltpu.VMEM((chips // 2,) + block, bf16),
            pltpu.VMEM((chips // 2,) + block, bf16),
            pltpu.SemaphoreType.DMA((3, chips)),
            pltpu.SemaphoreType.DMA((3, chips)),
        ],
        compiler_params=params(number),
    )(part)


def shards(devices, tokens, w_qkv, w_out, w_in, w_down, gain_attn, gain_mlp, cotangent):
    rows, wide = tokens.shape
    own = w_qkv.shape[0]
    scale = HEAD_DIM ** (-0.5)
    width_here = w_qkv.shape[2]
    hidden_here = w_in.shape[2]
    sizes = (3 * width_here, 2 * hidden_here, width_here, hidden_here, 1, 1)
    marks = [sum(sizes[:i]) for i in range(len(sizes) + 1)]
    spare = -marks[-1] % 128
    packed = jnp.concatenate(
        [
            w_qkv.reshape(own, -1),
            w_in.reshape(own, -1),
            w_out.T,
            w_down.T,
            gain_attn[:, None],
            gain_mlp[:, None],
            jnp.zeros((own, spare), bf16),
        ],
        axis=1,
    )
    everything = all_gather(packed, devices, 0).reshape(wide, -1)
    full_qkv, full_in, out_turned, down_turned = (
        everything[:, marks[i] : marks[i + 1]] for i in range(4)
    )
    gain_first = everything[:, marks[4]].astype(f32)
    gain_second = everything[:, marks[5]].astype(f32)
    cosine, sine = rope_tables(lax.axis_index("ctx") * rows, rows)
    inputs = tokens.astype(f32)
    normed = layer_norm(inputs, gain_first).astype(bf16)
    mixed_qkv = nn(normed, full_qkv).reshape(rows, 3, width_here)
    query_heads = rotate(split_heads(mixed_qkv[:, 0]), cosine, sine).astype(bf16)
    key_heads = rotate(split_heads(mixed_qkv[:, 1]), cosine, sine).astype(bf16)
    query_rows = query_heads.reshape(rows, width_here) * jnp.asarray(scale, bf16)
    kv = jnp.concatenate(
        [key_heads.reshape(rows, width_here), mixed_qkv[:, 2].astype(bf16)], axis=1
    )
    kv_all, attended, log_total = forward_attention(query_rows, kv, devices, 1)
    attended_low = attended.astype(bf16)
    branch = head_sum(nt(attended_low, out_turned), 2)
    middle = inputs + branch
    normed_mlp, second_pull = jax.vjp(layer_norm, middle, gain_second)
    normed_mlp = normed_mlp.astype(bf16)
    gate_up = nn(normed_mlp, full_in).reshape(rows, 2, hidden_here)

    def activate(first, second):
        return jax.nn.gelu(first, approximate=False) * second

    hidden_values, activate_pull = jax.vjp(activate, gate_up[:, 0], gate_up[:, 1])
    hidden = hidden_values.astype(bf16)
    grad_hidden = nn(cotangent, down_turned)
    grad_pair = jnp.concatenate(activate_pull(grad_hidden), axis=1).astype(bf16)
    sums = head_sum(
        jnp.concatenate([nt(hidden, down_turned), nt(grad_pair, full_in)], axis=1), 3
    )
    mixed = (middle + sums[:, :wide]).astype(bf16)
    grad_middle_norm, grad_gain_mlp = second_pull(sums[:, wide:])
    grad_middle = cotangent.astype(f32) + grad_middle_norm
    grad_attn = grad_middle.astype(bf16)
    grad_rows = nn(grad_attn, out_turned).astype(bf16)
    correction = jnp.sum(split_heads(grad_rows.astype(f32) * attended), axis=2)
    heads_here = width_here // HEAD_DIM
    stats = jnp.concatenate(
        [log_total, correction.T, jnp.zeros((8 - heads_here, rows), f32)], axis=0
    )
    grad_query, grad_key, grad_value = backward_attention(
        jnp.concatenate([query_rows, grad_rows], axis=1), stats, kv, kv_all, devices, 4
    )
    grad_query = unrotate(split_heads(grad_query), cosine, sine).reshape(rows, width_here)
    grad_key = unrotate(split_heads(grad_key), cosine, sine).reshape(rows, width_here)
    grad_triple = jnp.concatenate([grad_query, grad_key, grad_value], axis=1).astype(bf16)
    grad_normed = head_sum(nt(grad_triple, full_qkv), 5)
    _, first_pull = jax.vjp(layer_norm, inputs, gain_first)
    grad_input_norm, grad_gain_attn = first_pull(grad_normed)
    grad_tokens = grad_middle + grad_input_norm

    def tn(a, b):
        return lax.dot_general(a, b, (((0,), (0,)), ((), ())), preferred_element_type=f32)

    parts = jnp.concatenate(
        [
            tn(normed, grad_triple).astype(bf16),
            tn(normed_mlp, grad_pair).astype(bf16),
            tn(grad_attn, attended_low).astype(bf16),
            tn(cotangent, hidden).astype(bf16),
            grad_gain_attn[:, None].astype(bf16),
            grad_gain_mlp[:, None].astype(bf16),
            jnp.zeros((wide, spare), bf16),
        ],
        axis=1,
    ).reshape(devices, own, -1)
    owned = reduce_scatter(parts, devices, 6)
    cut = [owned[:, marks[i] : marks[i + 1]] for i in range(6)]
    return (
        mixed,
        grad_tokens,
        cut[0].reshape(own, 3, width_here),
        cut[2].T,
        cut[1].reshape(own, 2, hidden_here),
        cut[3].T,
        cut[4][:, 0],
        cut[5][:, 0],
    )


def solution(mesh):
    in_specs = (
        P("ctx", None),
        P("ctx", None, "head"),
        P("head", "ctx"),
        P("ctx", None, "head"),
        P("head", "ctx"),
        P("ctx"),
        P("ctx"),
        P("ctx", None),
    )
    out_specs = (
        P("ctx", None),
        P("ctx", None),
        P("ctx", None, "head"),
        P("head", "ctx"),
        P("ctx", None, "head"),
        P("head", "ctx"),
        P("ctx"),
        P("ctx"),
    )
    return jax.shard_map(
        functools.partial(shards, mesh.shape["ctx"]),
        mesh=mesh, in_specs=in_specs, out_specs=out_specs, check_vma=False,
    )
```

time: 794 us -> 316 us (0.40)
  waiting for transfers between devices: 349 us -> 0 us
  Pallas kernels: 0 us -> 233 us
  blocking collectives: 157 us -> 0 us
  matrix products: 139 us -> 22.3 us
  local copies, waits for them, and re-layouts: 96.4 us -> 35.3 us
  between operations: 16 us -> 1.31 us
    pallas_call x0 -> x7, Pallas kernels: none -> 233 us  [the longest x1 55.6 us: backward_attention(): pl.pallas_call(functools.partial(backward_kernel, devices, heads), out_sh...]
    reduce_scatter x4 -> x0, waiting for transfers between devices: 157 us -> none  [the longest x1 71.5 us: shards(): lax.psum_scatter(grad_qkv, 'ctx', scatter_dimension=0, tiled=True)]
    dot_general x68 -> x12, matrix products: 139 us -> 22.3 us  [the longest x4 9.4 us: nt(): lax.dot_general(a, b, (((1,), (1,)), ((), ())), preferred_element_type=f32)]
    all_gather x6 -> x0, waiting for transfers between devices: 109 us -> none  [the longest x1 42.4 us: shards(): lax.all_gather(w_in, 'ctx', axis=0, tiled=True)]
    all_gather x4 -> x0, blocking collectives: 87.5 us -> none  [the longest x1 23.2 us: shards(): lax.all_gather(log_total, 'ctx', axis=0, tiled=True)]
    psum x3 -> x0, waiting for transfers between devices: 81.9 us -> none  [the longest x1 40.5 us: shards(): lax.psum(jnp.dot(hidden, full_down, preferred_element_type=jnp.float32),...]
    unnamed x2 -> x0, blocking collectives: 69.5 us -> none
    dynamic_slice x40 -> x0, local copies, waits for them, and re-layouts: 51.2 us -> none  [in_blocks(): state, _ = lax.scan(advance, state, stacked)]
  transfers between devices with their start and end apart: 13 -> 0, of which waited for: 10 -> 0; matrix products, arithmetic and copies ran while one was open for 26% -> 0% of each run, Pallas kernels for 0% -> 0%
where the time goes in v1:
time: 316 us; the launch traced here: 314 us
  Pallas kernels  233 us (74%)
  local copies, waits for them, and re-layouts  35.3 us (11%)
  other arithmetic  22.5 us (7%)
  matrix products  22.3 us (7%)
    pallas_call x1, Pallas kernels, backward_attention(): pl.pallas_call(functools.partial(backward_kernel, devices, heads), out_sh...  55.6 us
    pallas_call x1, Pallas kernels, forward_attention(): pl.pallas_call(functools.partial(forward_kernel, devices, heads), out_sha...  47.2 us
    pallas_call x3, Pallas kernels, head_sum(): pl.pallas_call(exchange_kernel, out_shape=jax.ShapeDtypeStruct(part.shape...  45.9 us
    pallas_call x1, Pallas kernels, reduce_scatter(): pl.pallas_call(functools.partial(scatter_kernel, devices), out_shape=jax....  42.9 us
    pallas_call x1, Pallas kernels, all_gather(): pl.pallas_call(functools.partial(gather_kernel, devices), out_shape=jax.S...  41.3 us
    dot_general x4, matrix products, nt(): lax.dot_general(a, b, (((1,), (1,)), ((), ())), preferred_element_type=f32)  9.4 us
    dot_general x4, matrix products, nn(): return jnp.dot(a, b, preferred_element_type=f32)  8.26 us
    concatenate x1, local copies, waits for them, and re-layouts, shards(): jnp.concatenate([tn(normed, grad_triple).astype(bf16), tn(normed_mlp, gra...  7.92 us

profile of v1, /device:TPU:0, one launch (start us, length us, event | category | flops | bytes accessed | tf_op | source)
XLA Modules:
  0.0 314.4 jit_solution(12259502267345772237)
XLA Ops:
  0.6 0.9 copy.58
  1.5 1.0 reshape.245
  2.6 0.8 copy.24
  3.3 0.8 copy.25
  4.1 1.7 concatenate.59.own
  5.8 41.3 %shard_map.143 = bf16[16,48,3328]{2,1,0:T(8,128)(2,1)} custom-call(bf16[48,3328]{1,0:T(8,128)(2,1)} %concatenate.59.own), custom_call_target="tpu_custom_call" | custom-call | tf_op jit(solution)/shard_map/pallas_call | solution.py:212
  47.1 1.2 fusion.71
  48.7 0.2 fusion.25
  48.9 2.4 fusion.6
  51.3 1.0 copy-done.14
  52.8 0.6 copy-done.15
  53.6 0.2 copy.29
  53.9 0.7 fusion.54.q
  54.6 1.0 slice.117
  55.8 0.2 copy.35
  56.0 0.2 copy.55
  56.2 0.8 pad_maximum_fusion.3.kv
  57.0 47.2 %shard_map.144 = (bf16[16,256,768]{2,1,0:T(8,128)(2,1)}, f32[256,384]{1,0:T(8,128)}, f32[8,256]{1,0:T(8,128)}) custom-call(bf16[256,384]{1,0:T(8,128)(2,1)} %fusion.54.q, bf16[256,768]{1,0:T(8,128)(2,1)} %pad_maximum_fusion.3.kv), custom_call_target="tpu_custom_call" | custom-call | tf_op jit(solution)/shard_map/pallas_call | solution.py:323
  104.3 2.3 convolution_convert_fusion.5.own
  106.6 12.9 %shard_map.145 = f32[256,768]{1,0:T(8,128)} custom-call(bf16[256,768]{1,0:T(8,128)(2,1)} %convolution_convert_fusion.5.own), custom_call_target="tpu_custom_call" | custom-call | tf_op jit(solution)/shard_map/pallas_call | solution.py:487
  119.5 1.3 fusion.70
  121.0 0.2 multiply_reduce_fusion.2
  121.2 2.4 fusion.2
  123.6 1.3 multiply_convert_fusion.2
  124.9 2.0 fusion.34
  126.9 2.4 fusion.12
  129.4 1.7 convolution_convert_fusion.4
  131.1 0.9 pad_maximum_fusion.own
  132.0 21.0 %shard_map.146 = f32[256,1536]{1,0:T(8,128)} custom-call(bf16[256,1536]{1,0:T(8,128)(2,1)} %pad_maximum_fusion.own), custom_call_target="tpu_custom_call" | custom-call | tf_op jit(solution)/shard_map/pallas_call | solution.py:487
  153.0 2.1 multiply_reduce_fusion
  155.2 1.1 fusion.68
  156.3 0.6 copy-done.27
  157.0 1.6 convert_multiply_fusion
  158.6 0.8 pad_maximum_fusion.4.qg
  159.7 1.4 maximum_maximum_fusion.stats
  161.1 55.6 %shard_map.147 = (f32[256,384]{1,0:T(8,128)}, f32[256,384]{1,0:T(8,128)}, f32[256,384]{1,0:T(8,128)}) custom-call(bf16[256,768]{1,0:T(8,128)(2,1)} %pad_maximum_fusion.4.qg, f32[16,256]{1,0:T(8,128)} %maximum_maximum_fusion.stats, bf16[256,768]{1,0:T(8,128)(2,1)} %pad_maximum_fusion.3.kv, bf16[16,256,768]{2,1,0:T(8,128)(2,1)} %get-tuple-element.16.kv_all), custom_call_target="tpu_custom_call" | custom-call | tf_op jit(solution)/shard_map/pallas_call | solution.py:439
  216.7 1.7 convert.33
  218.4 1.2 copy.41
  219.6 0.8 slice_negate_fusion.1
  220.6 2.0 maximum_multiply_fusion.2
  222.7 1.9 copy.42
  224.6 1.9 copy.45
  226.5 1.3 subtract_convert_fusion.1
  227.8 2.9 fusion.9.own
  230.7 12.0 %shard_map.148 = f32[256,768]{1,0:T(8,128)} custom-call(bf16[256,768]{1,0:T(8,128)(2,1)} %fusion.9.own), custom_call_target="tpu_custom_call" | custom-call | tf_op jit(solution)/shard_map/pallas_call | solution.py:487
  242.7 1.5 fusion.26
  244.2 2.1 fusion.24
  246.4 1.3 add_add_fusion.2
  247.7 2.1 convolution_convert_fusion.1
  249.8 0.8 convolution_convert_fusion
  250.9 0.4 convolution_convert_fusion.3
  251.3 1.3 fusion.8
  252.6 1.5 copy.46
  254.2 0.3 convert_element_type.162
  254.6 1.0 convert_element_type.163
  255.6 0.7 broadcast_in_dim.49
  256.3 7.9 %concatenate.75.part = bf16[16,48,3328]{2,1,0:T(8,128)(2,1)} concatenate(bf16[16,48,1152]{2,1,0:T(8,128)(2,1)} %bitcast.156, bf16[16,48,1152]{2,1,0:T(8,128)(2,1)S(1)} %bitcast.149, bf16[16,48,384]{2,1,0:T(8,128)(2,1)S(1)} %bitcast.155, bf16[16,48,576]{2,1,0:T(8,128)(2,1)S(1)} %bitcast.152, bf16[16,48,1]{2,1,0:T(8,128)(2,1)S(1)} %convert_element_type.162, ...), dimensions={2} | concatenate | bytes 10223616 | tf_op jit(solution)/shard_map/concatenate | solution.py:663
  264.2 42.9 %shard_map.149 = f32[48,3328]{1,0:T(8,128)} custom-call(bf16[16,48,3328]{2,1,0:T(8,128)(2,1)} %concatenate.75.part), custom_call_target="tpu_custom_call" | custom-call | tf_op jit(solution)/shard_map/pallas_call | solution.py:568
  307.1 1.1 fusion.73
  308.2 0.7 copy.60
  308.9 1.5 slice_bitcast_fusion.2
  310.4 0.9 reshape.253
  311.3 1.6 slice_bitcast_fusion.1
  312.9 1.5 slice_reduce_fusion
  (92 shorter events, 2.4 us)
Async XLA Ops:
  5.8 42.7 %copy-start = (bf16[256,768]{1,0:T(8,128)(2,1)S(1)}, bf16[256,768]{1,0:T(8,128)(2,1)}, u32[]{:S(2)}) copy-start(bf16[256,768]{1,0:T(8,128)(2,1)} %param.8) | copy-start | bytes 1179652
  48.9 2.4 copy-start.25
  48.9 2.4 copy-start.23
  51.3 1.0 copy-start.14
  52.7 0.6 copy-start.15
  121.2 34.0 %copy-start.21 = (f32[256]{0:T(256)}, f32[256]{0:T(256)S(1)}, u32[]{:S(2)}) copy-start(f32[256]{0:T(256)S(1)} %fusion.60) | copy-start | bytes 3076
  123.6 1.3 copy-start.3
  124.9 4.5 %copy-start.12 = (bf16[256,576]{0,1:T(8,128)(2,1)}, bf16[256,576]{0,1:T(8,128)(2,1)S(1)}, u32[]{:S(2)}) copy-start(bf16[256,576]{0,1:T(8,128)(2,1)S(1)} %get-tuple-element.44) | copy-start | bytes 884740
  126.9 2.5 copy-start.16
  126.9 2.5 copy-start.18
  153.0 2.2 copy-start.2
  155.2 1.8 copy-start.5
  156.3 0.6 copy-start.27
  156.8 1.8 copy-start.9
  157.0 1.6 copy-start.7
  216.7 3.7 %copy-start.11 = (f32[256,384]{1,0:T(8,128)S(1)}, f32[256,384]{1,0:T(8,128)}, u32[]{:S(2)}) copy-start(f32[256,384]{1,0:T(8,128)} %get-tuple-element.18) | copy-start | bytes 1179652
  220.6 5.9 %copy-start.10 = (f32[256,384]{1,0:T(8,128)S(1)}, f32[256,384]{1,0:T(8,128)}, u32[]{:S(2)}) copy-start(f32[256,384]{1,0:T(8,128)} %get-tuple-element.17) | copy-start | bytes 1179652
  226.5 1.3 copy-start.20
  230.7 13.5 %copy-start.26 = (f32[256]{0:T(256)S(1)}, f32[256]{0:T(256)}, u32[]{:S(2)}) copy-start(f32[256]{0:T(256)} %copy-done.25) | copy-start | bytes 3076
  230.7 13.5 %copy-start.24 = (f32[256]{0:T(256)S(1)}, f32[256]{0:T(256)}, u32[]{:S(2)}) copy-start(f32[256]{0:T(256)} %copy-done.23) | copy-start | bytes 3076
  230.7 15.7 %copy-start.28 = (f32[256]{0:T(256)S(1)}, f32[256]{0:T(256)}, u32[]{:S(2)}) copy-start(f32[256]{0:T(256)} %copy-done.27) | copy-start | bytes 3076
  242.7 3.7 %copy-start.1 = (f32[256,768]{1,0:T(8,128)S(1)}, f32[256,768]{1,0:T(8,128)}, u32[]{:S(2)}) copy-start(f32[256,768]{1,0:T(8,128)} %shard_map.148) | copy-start | bytes 2359300
  247.7 2.1 copy-start.17
  247.7 2.1 copy-start.19
  247.7 2.1 copy-start.22
  249.8 1.0 copy-start.6
  249.8 1.1 copy-start.8
  249.8 1.5 copy-start.4
  249.8 1.5 copy-start.13
  251.3 2.9 copy-start.30
  251.3 3.2 %copy-start.29 = (bf16[768]{0:T(1024)(128)(2,1)S(1)}, bf16[768]{0:T(1024)(128)(2,1)}, u32[]{:S(2)}) copy-start(bf16[768]{0:T(1024)(128)(2,1)} %get-tuple-element.36) | copy-start | bytes 4612

commit v2 on v1

v2 whole, which is shorter than its diff:
```python
import functools

import jax
import jax.numpy as jnp
from jax import lax
from jax.experimental import pallas as pl
from jax.experimental.pallas import tpu as pltpu
from jax.sharding import PartitionSpec as P

HEAD_DIM = 64
PAIR = 2 * HEAD_DIM
MESH = pl.DeviceIdType.MESH
VMEM_LIMIT = 56 * 1024 * 1024
RESIDENT_LIMIT = 32 * 1024 * 1024

rope_base = 160000.0
epsilon = 1e-05
f32 = jnp.float32
bf16 = jnp.bfloat16


def layer_norm(values, gain):
    centred = values - jnp.mean(values, axis=-1, keepdims=True)
    spread = jnp.mean(centred * centred, axis=-1, keepdims=True)
    return centred * lax.rsqrt(spread + epsilon) * gain


def rope_tables(first, rows):
    positions = (first + jnp.arange(rows, dtype=jnp.int32)).astype(f32)
    exponent = jnp.arange(HEAD_DIM // 2, dtype=jnp.int32).astype(f32) * (2.0 / HEAD_DIM)
    inverse = rope_base ** (-exponent)
    angles = positions[:, None] * inverse[None, :]
    angles = jnp.concatenate([angles, angles], axis=1)[:, None, :]
    return (jnp.cos(angles), jnp.sin(angles))


def turn_half(values):
    half = values.shape[-1] // 2
    return jnp.concatenate([-values[..., half:], values[..., :half]], axis=-1)


def rotate(values, cosine, sine):
    return values * cosine + turn_half(values) * sine


def unrotate(values, cosine, sine):
    return values * cosine - turn_half(values) * sine


def split_heads(flat_rows):
    return flat_rows.reshape(flat_rows.shape[0], -1, HEAD_DIM)


class Ring:
    def __init__(self, devices):
        self.chips = devices // 2
        self.half = self.chips // 2
        self.me = lax.axis_index("ctx")
        self.head = lax.axis_index("head")
        chip = lax.div(self.me, 2)
        self.core = lax.rem(self.me, 2)
        side = lax.rem(chip, 2)
        level = lax.div(chip, 2)
        self.place = level + side * (self.chips - 1 - 2 * level)

    def chip_at(self, place):
        place = lax.rem(place + 2 * self.chips, self.chips)
        far = lax.div(place, self.chips // 2)
        return (1 - far) * 2 * place + far * (2 * (self.chips - 1 - place) + 1)

    def index(self, offset, core):
        return self.chip_at(self.place + offset) * 2 + core

    def neighbours(self):
        return (self.index(1, self.core), self.index(-1, self.core), self.me + 1 - 2 * self.core)

    def barrier(self, across=False):
        sem = pltpu.get_barrier_semaphore()
        for other in self.neighbours():
            pl.semaphore_signal(sem, inc=1, device_id=(other, self.head), device_id_type=MESH)
        if across:
            pl.semaphore_signal(
                sem, inc=1, device_id=(self.me, 1 - self.head), device_id_type=MESH
            )
        pl.semaphore_wait(sem, 4 if across else 3)


def turns(ring, which):
    return (ring.half, ring.half - 1) if which % 2 == 0 else (ring.half - 1, ring.half)


class Gather:
    def __init__(self, ring, own, full, send, recv, local):
        self.ring, self.own, self.full = ring, own, full
        self.send, self.recv, self.local = send, recv, local
        self.right, self.left, self.sibling = ring.neighbours()

    def copy(self, a, kind, number, slot, target, first=False):
        return pltpu.make_async_remote_copy(
            src_ref=self.own[a] if first else self.full[a].at[slot],
            dst_ref=self.full[a].at[slot],
            send_sem=self.send.at[a, kind, number],
            recv_sem=self.recv.at[a, kind, number],
            device_id=(target, self.ring.head),
            device_id_type=MESH,
        )

    def arrive(self, a, kind, number, slot):
        self.copy(a, kind, number, slot, self.sibling).wait_recv()

    def begin(self):
        ring = self.ring
        locals_ = []
        for a in range(len(self.own)):
            rights, lefts = turns(ring, a)
            if rights:
                self.copy(a, 0, 0, ring.me, self.right, True).start()
            if lefts:
                self.copy(a, 1, 0, ring.me, self.left, True).start()
            self.copy(a, 2, 0, ring.me, self.sibling, True).start()
        for a in range(len(self.own)):
            copy = pltpu.make_async_copy(
                self.own[a], self.full[a].at[ring.me], self.local.at[a]
            )
            copy.start()
            locals_.append(copy)
        for copy in locals_:
            copy.wait()

    def step(self, s):
        ring = self.ring

        def onward(a, kind, hops, number, offset, target):
            @pl.when(s <= hops)
            def _():
                slot = ring.index(offset, ring.core)
                self.arrive(a, kind, s - 1, slot)

                @pl.when(s < hops)
                def _():
                    self.copy(a, kind, s, slot, target).start()

                self.copy(a, 2, number, slot, self.sibling).start()

        for a in range(len(self.own)):
            rights, lefts = turns(ring, a)
            onward(a, 0, rights, s, -s, self.right)
            onward(a, 1, lefts, rights + s, s, self.left)

    def sibling_step(self, s):
        ring = self.ring

        def come(a, hops, number, offset):
            @pl.when(s <= hops)
            def _():
                self.arrive(a, 2, number, ring.index(offset, 1 - ring.core))

        for a in range(len(self.own)):
            rights, lefts = turns(ring, a)
            come(a, rights, s, -s)
            come(a, lefts, rights + s, s)

    def sibling_first(self):
        for a in range(len(self.own)):
            self.arrive(a, 2, 0, self.sibling)

    def finish(self):
        ring = self.ring

        def sent(a, kind):
            def one(number, carry):
                self.copy(a, kind, number, ring.me, self.sibling).wait_send()
                return carry

            return one

        for a in range(len(self.own)):
            rights, lefts = turns(ring, a)
            lax.fori_loop(0, rights, sent(a, 0), 0)
            lax.fori_loop(0, lefts, sent(a, 1), 0)
            lax.fori_loop(0, ring.chips, sent(a, 2), 0)


class Scatter:
    def __init__(self, ring, parts, outs, stages, froms, send, recv):
        self.ring, self.parts, self.outs = ring, parts, outs
        self.stages, self.froms = stages, froms
        self.send, self.recv = send, recv
        self.right, self.left, self.sibling = ring.neighbours()

    def make(self, a, source, target, kind, number, device):
        return pltpu.make_async_remote_copy(
            src_ref=source, dst_ref=target,
            send_sem=self.send.at[a, kind, number], recv_sem=self.recv.at[a, kind, number],
            device_id=(device, self.ring.head), device_id_type=MESH,
        )

    def chip(self, a, kind, s):
        rights, lefts = turns(self.ring, a)
        return self.ring.chip_at(self.ring.place + ((rights - s) if kind == 0 else (s - lefts)))

    def over(self, a, chip):
        ring = self.ring
        return self.make(
            a, self.parts[a].at[chip * 2 + 1 - ring.core], self.stages[a].at[chip], 2, chip,
            self.sibling,
        )

    def here(self, a, chip):
        self.over(a, chip).wait_recv()
        return self.stages[a][chip].astype(f32) + self.parts[a][
            chip * 2 + self.ring.core
        ].astype(f32)

    def begin(self):
        def launch(s, carry):
            for a in range(len(self.parts)):
                for kind in range(2):
                    @pl.when(s < turns(self.ring, a)[kind])
                    def _():
                        self.over(a, self.chip(a, kind, s)).start()

            return carry

        lax.fori_loop(0, self.ring.half, launch, 0)
        for a in range(len(self.parts)):
            self.over(a, self.ring.chip_at(self.ring.place)).start()

    def first(self):
        for a in range(len(self.parts)):
            for kind in range(2):
                if turns(self.ring, a)[kind]:
                    chip = self.chip(a, kind, 0)
                    self.stages[a][chip] = self.here(a, chip).astype(bf16)
                    self.make(
                        a, self.stages[a].at[chip], self.froms[a].at[kind, 0], kind, 0,
                        (self.right, self.left)[kind],
                    ).start()

    def landed(self, a, kind, number):
        ref = self.froms[a].at[kind, number]
        self.make(a, ref, ref, kind, number, self.right).wait_recv()
        return self.froms[a][kind, number].astype(f32)

    def step(self, s):
        def onward(a, kind):
            @pl.when(s < turns(self.ring, a)[kind])
            def _():
                own = self.here(a, self.chip(a, kind, s))
                total = own + self.landed(a, kind, s - 1)
                self.froms[a][kind, s - 1] = total.astype(bf16)
                self.make(
                    a, self.froms[a].at[kind, s - 1], self.froms[a].at[kind, s], kind, s,
                    (self.right, self.left)[kind],
                ).start()

        for a in range(len(self.parts)):
            for kind in range(2):
                onward(a, kind)

    def last(self):
        ring = self.ring
        for a in range(len(self.parts)):
            total = self.here(a, ring.chip_at(ring.place))
            for kind in range(2):
                hops = turns(ring, a)[kind]
                if hops:
                    total = total + self.landed(a, kind, hops - 1)
            self.outs[a][...] = total

    def finish(self):
        def sent(a, kind):
            def one(number, carry):
                ref = self.froms[a].at[0, 0]
                self.make(a, ref, ref, kind, number, self.right).wait_send()
                return carry

            return one

        for a in range(len(self.parts)):
            for kind in range(2):
                lax.fori_loop(0, turns(self.ring, a)[kind], sent(a, kind), 0)
            lax.fori_loop(0, self.ring.chips, sent(a, 2), 0)


def scatter_scratch(parts, devices):
    chips = devices // 2
    count = len(parts)
    return (
        [pltpu.VMEM((chips,) + part.shape[1:], bf16) for part in parts]
        + [pltpu.VMEM((2, chips // 2) + part.shape[1:], bf16) for part in parts]
        + [pltpu.SemaphoreType.DMA((count, 3, chips)), pltpu.SemaphoreType.DMA((count, 3, chips))]
    )


def gather_sems(arrays, devices):
    chips = devices // 2
    return [
        pltpu.SemaphoreType.DMA((arrays, 3, chips)),
        pltpu.SemaphoreType.DMA((arrays, 3, chips)),
        pltpu.SemaphoreType.DMA((arrays,)),
    ]


def params(number):
    return pltpu.CompilerParams(
        collective_id=number, has_side_effects=True, vmem_limit_bytes=VMEM_LIMIT
    )


whole_vmem = pl.BlockSpec(memory_space=pltpu.VMEM)
whole_any = pl.BlockSpec(memory_space=pl.ANY)


def gather_kernel(devices, count, *refs):
    ring = Ring(devices)
    ring.barrier()
    gather = Gather(ring, refs[:count], refs[count : 2 * count], *refs[2 * count :])
    gather.begin()
    gather.sibling_first()

    def step(s, carry):
        gather.step(s)
        return carry

    lax.fori_loop(1, ring.half + 1, step, 0)

    def late(s, carry):
        gather.sibling_step(s)
        return carry

    lax.fori_loop(1, ring.half + 1, late, 0)
    gather.finish()


def all_gather(own, devices, number):
    return pl.pallas_call(
        functools.partial(gather_kernel, devices, len(own)),
        out_shape=tuple(jax.ShapeDtypeStruct((devices,) + x.shape, x.dtype) for x in own),
        in_specs=[whole_any] * len(own),
        out_specs=tuple([whole_any] * len(own)),
        scratch_shapes=gather_sems(len(own), devices),
        compiler_params=params(number),
    )(*own)


def nt(a, b):
    return lax.dot_general(a, b, (((1,), (1,)), ((), ())), preferred_element_type=f32)


def nn(a, b):
    return jnp.dot(a, b, preferred_element_type=f32)


def lane_mask(rows, side):
    lanes = lax.broadcasted_iota(jnp.int32, (rows, PAIR), 1)
    return (lanes >= HEAD_DIM) if side else (lanes < HEAD_DIM)


def masked_heads(source, offset, heads, target):
    for h in range(heads):
        start = offset + (h // 2) * PAIR
        block = source[:, start : start + PAIR].astype(f32)
        keep = lane_mask(block.shape[0], h % 2)
        target[h] = jnp.where(keep, block, 0.0).astype(bf16)


def fetch(sources, targets, sems):
    copies = [
        pltpu.make_async_copy(source, target, sems.at[i])
        for i, (source, target) in enumerate(zip(sources, targets))
    ]
    for copy in copies:
        copy.start()
    for copy in copies:
        copy.wait()


def visit(ring, gather, process, scatter=None):
    gather.begin()
    if scatter:
        scatter.begin()
        scatter.first()

    def opening(other, carry):
        @pl.when(other == 1)
        def _():
            gather.sibling_first()

        process(ring.index(0, ring.core + other * (1 - 2 * ring.core)))
        return carry

    lax.fori_loop(0, 2, opening, 0)

    def step(s, carry):
        gather.step(s)

        def half(other, carry):
            @pl.when(other == 1)
            def _():
                gather.sibling_step(s)
                if scatter:
                    @pl.when(s < ring.half)
                    def _():
                        scatter.step(s)

            core = ring.core + other * (1 - 2 * ring.core)
            ways = jnp.where(s < ring.half, 2, 1)

            def way(w, carry):
                process(ring.index((2 * w - 1) * s, core))
                return carry

            return lax.fori_loop(0, ways, way, carry)

        return lax.fori_loop(0, 2, half, carry)

    lax.fori_loop(1, ring.half + 1, step, 0)
    gather.finish()
    if scatter:
        scatter.last()
        scatter.finish()


def forward_kernel(
    devices, heads, q, k, v, full_k, full_v, att, lse, qm, top, total, acc, send, recv, local, *stage
):
    ring = Ring(devices)
    ring.barrier()
    gather = Gather(ring, [k, v], [full_k, full_v], send, recv, local)
    masked_heads(q, 0, heads, qm)
    top[...] = jnp.full_like(top, -1e30)
    total[...] = jnp.zeros_like(total)
    acc[...] = jnp.zeros_like(acc)

    def process(slot):
        keyed, valued = full_k.at[slot], full_v.at[slot]
        if stage:
            fetch((keyed, valued), stage[:2], stage[2])
            keyed, valued = stage[:2]
        for p in range(heads // 2):
            keys = keyed[:, p * PAIR : (p + 1) * PAIR]
            values = valued[:, p * PAIR : (p + 1) * PAIR].T
            for side in range(2):
                h = 2 * p + side
                scores = nt(keys, qm[h])
                before = top[h : h + 1]
                peak = jnp.maximum(before, jnp.max(scores, axis=0, keepdims=True))
                shrink = jnp.exp(before - peak)
                weights = jnp.exp(scores - peak)
                top[h : h + 1] = peak
                total[h : h + 1] = total[h : h + 1] * shrink + jnp.sum(
                    weights, axis=0, keepdims=True
                )
                part = nn(values[side * HEAD_DIM : (side + 1) * HEAD_DIM], weights.astype(bf16))
                rows = slice(h * HEAD_DIM, (h + 1) * HEAD_DIM)
                acc[rows] = acc[rows] * shrink + part

    visit(ring, gather, process)
    for h in range(heads):
        rows = slice(h * HEAD_DIM, (h + 1) * HEAD_DIM)
        acc[rows] = acc[rows] / total[h : h + 1]
    att[...] = acc[...].T
    lse[...] = top[...] + jnp.log(jnp.maximum(total[...], 1e-37))


def resident(devices, rows, width):
    return devices * rows * width * 2 * 2 <= RESIDENT_LIMIT


def forward_attention(q, k, v, devices, number):
    rows, width = q.shape
    heads = width // HEAD_DIM
    near = resident(devices, rows, 2 * width)
    space = whole_vmem if near else whole_any
    full = jax.ShapeDtypeStruct((devices,) + k.shape, bf16)
    return pl.pallas_call(
        functools.partial(forward_kernel, devices, heads),
        out_shape=(
            full,
            full,
            jax.ShapeDtypeStruct((rows, width), f32),
            jax.ShapeDtypeStruct((8, rows), f32),
        ),
        in_specs=[whole_vmem, space, space],
        out_specs=(space, space, whole_vmem, whole_vmem),
        scratch_shapes=[
            pltpu.VMEM((heads, rows, PAIR), bf16),
            pltpu.VMEM((8, rows), f32),
            pltpu.VMEM((8, rows), f32),
            pltpu.VMEM((width, rows), f32),
        ]
        + gather_sems(2, devices)
        + (
            []
            if near
            else [
                pltpu.VMEM(k.shape, bf16),
                pltpu.VMEM(v.shape, bf16),
                pltpu.SemaphoreType.DMA((2,)),
            ]
        ),
        compiler_params=params(number),
    )(q, k, v)


def unturn(block, cosine, sine):
    half = HEAD_DIM // 2
    low, high = block[:half], block[half:]
    return jnp.concatenate(
        [low * cosine + high * sine, high * cosine - low * sine], axis=0
    )


def backward_kernel(devices, heads, near, count, *refs):
    q, g, stats, k, v, k_all, v_all, cosine, sine, lonely = refs[:10]
    parts = refs[10 : 10 + count]
    rest = refs[10 + count :]
    triple, joined = rest[:2]
    outs = rest[2 : 2 + count]
    rest = rest[2 + count :]
    q_all, g_all, stats_all = rest[:3]
    qm, gm, km, vm, dqt, dka, dva, send, recv, local = rest[3:13]
    stages = rest[13 : 13 + count]
    froms = rest[13 + count : 13 + 2 * count]
    scatter_send, scatter_recv, met, met_send, met_recv = rest[13 + 2 * count : 18 + 2 * count]
    stage = rest[18 + 2 * count :]
    width = heads * HEAD_DIM
    ring = Ring(devices)
    ring.barrier(True)
    meet = pltpu.make_async_remote_copy(
        src_ref=lonely, dst_ref=met, send_sem=met_send, recv_sem=met_recv,
        device_id=(ring.me, 1 - ring.head), device_id_type=MESH,
    )
    meet.start()
    gather = Gather(ring, [q, g, stats], [q_all, g_all, stats_all], send, recv, local)
    scatter = Scatter(ring, parts, outs, stages, froms, scatter_send, scatter_recv)
    own_q, own_g, mine = q, g, stats
    if stage:
        fetch((q, g, stats), (stage[0], stage[1], stage[6]), stage[5])
        own_q, own_g, mine = stage[0], stage[1], stage[6]
    masked_heads(own_q, 0, heads, qm)
    masked_heads(own_g, 0, heads, gm)
    masked_heads(k, 0, heads, km)
    masked_heads(v, 0, heads, vm)
    dqt[...] = jnp.zeros_like(dqt)
    dka[...] = jnp.zeros_like(dka)
    dva[...] = jnp.zeros_like(dva)

    def process(slot):
        asked, graded, rows_of = q_all.at[slot], g_all.at[slot], stats_all.at[slot]
        keyed, valued = k_all.at[slot], v_all.at[slot]
        if stage:
            fetch((asked, graded, rows_of, keyed, valued), stage[:5], stage[5])
            asked, graded, rows_of, keyed, valued = stage[:5]
        for p in range(heads // 2):
            span = slice(p * PAIR, (p + 1) * PAIR)
            keys = keyed[:, span]
            values = valued[:, span]
            turned = keys.T
            queries = asked[:, span]
            grads = graded[:, span]
            for side in range(2):
                h = 2 * p + side
                probs = jnp.exp(nt(keys, qm[h]) - mine[h : h + 1])
                slope = nt(values, gm[h])
                small = (probs * (slope - mine[8 + h : 9 + h])).astype(bf16)
                rows = slice(h * HEAD_DIM, (h + 1) * HEAD_DIM)
                dqt[rows] += nn(turned[side * HEAD_DIM : (side + 1) * HEAD_DIM], small)
                probs = jnp.exp(nt(km[h], queries) - rows_of[h : h + 1])
                slope = nt(vm[h], grads)
                small = (probs * (slope - rows_of[8 + h : 9 + h])).astype(bf16)
                dva[h] += nn(probs.astype(bf16), grads)
                dka[h] += nn(small, queries)

    visit(ring, gather, process, scatter)
    meet.wait()
    joined[...] = lonely[...].astype(f32) + met[...].astype(f32)
    keep = lane_mask(triple.shape[0], 0)
    scale = HEAD_DIM ** (-0.5)
    for p in range(heads // 2):
        for which in range(2):
            if which == 0:
                block = dqt[p * PAIR : (p + 1) * PAIR] * scale
            else:
                block = jnp.where(keep, dka[2 * p], dka[2 * p + 1]).T
            block = jnp.concatenate(
                [
                    unturn(block[:HEAD_DIM], cosine[...], sine[...]),
                    unturn(block[HEAD_DIM:], cosine[...], sine[...]),
                ],
                axis=0,
            )
            start = which * width + p * PAIR
            triple[:, start : start + PAIR] = block.T.astype(bf16)
        start = 2 * width + p * PAIR
        triple[:, start : start + PAIR] = jnp.where(keep, dva[2 * p], dva[2 * p + 1]).astype(bf16)


def backward_attention(q, g, stats, k, v, k_all, v_all, cosine, sine, lonely, parts, devices, number):
    rows, width = q.shape
    heads = width // HEAD_DIM
    near = resident(devices, rows, 2 * width)
    gathered = [(q.shape, bf16), (g.shape, bf16), (stats.shape, f32)]
    gathered = [((devices,) + shape, kind) for shape, kind in gathered]
    out_shape = [
        jax.ShapeDtypeStruct((rows, 3 * width), bf16),
        jax.ShapeDtypeStruct(lonely.shape, f32),
    ] + [jax.ShapeDtypeStruct(part.shape[1:], f32) for part in parts]
    out_specs = [whole_vmem] * len(out_shape)
    kept = len(out_shape)
    buffers = []
    if near:
        buffers = [pltpu.VMEM(shape, kind) for shape, kind in gathered]
    else:
        out_shape += [jax.ShapeDtypeStruct(shape, kind) for shape, kind in gathered]
        out_specs += [whole_any] * 3
    space = whole_vmem if near else whole_any
    return pl.pallas_call(
        functools.partial(backward_kernel, devices, heads, near, len(parts)),
        out_shape=tuple(out_shape),
        in_specs=[space] * 3 + [whole_vmem] * 2 + [space] * 2 + [whole_vmem] * (3 + len(parts)),
        out_specs=tuple(out_specs),
        scratch_shapes=buffers
        + [pltpu.VMEM((heads, rows, PAIR), bf16)] * 4
        + [
            pltpu.VMEM((width, rows), f32),
            pltpu.VMEM((heads, rows, PAIR), f32),
            pltpu.VMEM((heads, rows, PAIR), f32),
        ]
        + gather_sems(3, devices)
        + scatter_scratch(parts, devices)
        + [pltpu.VMEM(lonely.shape, bf16), pltpu.SemaphoreType.DMA, pltpu.SemaphoreType.DMA]
        + (
            []
            if near
            else [
                pltpu.VMEM(q.shape, bf16),
                pltpu.VMEM(g.shape, bf16),
                pltpu.VMEM(stats.shape, f32),
                pltpu.VMEM(k.shape, bf16),
                pltpu.VMEM(v.shape, bf16),
                pltpu.SemaphoreType.DMA((5,)),
                pltpu.VMEM(stats.shape, f32),
            ]
        ),
        compiler_params=params(number),
    )(q, g, stats, k, v, k_all, v_all, cosine, sine, lonely, *parts)[:kept]


def exchange_kernel(own, out, arrived, send, recv):
    other = 1 - lax.axis_index("head")
    here = lax.axis_index("ctx")
    sem = pltpu.get_barrier_semaphore()
    pl.semaphore_signal(sem, inc=1, device_id=(here, other), device_id_type=MESH)
    pl.semaphore_wait(sem, 1)
    copy = pltpu.make_async_remote_copy(
        src_ref=own, dst_ref=arrived, send_sem=send, recv_sem=recv,
        device_id=(here, other), device_id_type=MESH,
    )
    copy.start()
    copy.wait()
    out[...] = own[...].astype(f32) + arrived[...].astype(f32)


def head_sum(part, number):
    part = part.astype(bf16)
    return pl.pallas_call(
        exchange_kernel,
        out_shape=jax.ShapeDtypeStruct(part.shape, f32),
        in_specs=[whole_vmem],
        out_specs=whole_vmem,
        scratch_shapes=[
            pltpu.VMEM(part.shape, bf16), pltpu.SemaphoreType.DMA, pltpu.SemaphoreType.DMA,
        ],
        compiler_params=params(number),
    )(part)


def scatter_kernel(devices, count, *refs):
    ring = Ring(devices)
    ring.barrier()
    cut = [refs[i * count : (i + 1) * count] for i in range(4)]
    scatter = Scatter(ring, *cut, *refs[4 * count :])
    scatter.begin()
    scatter.first()

    def step(s, carry):
        scatter.step(s)
        return carry

    lax.fori_loop(1, ring.half, step, 0)
    scatter.last()
    scatter.finish()


def reduce_scatter(parts, devices, number):
    return pl.pallas_call(
        functools.partial(scatter_kernel, devices, len(parts)),
        out_shape=tuple(jax.ShapeDtypeStruct(part.shape[1:], f32) for part in parts),
        in_specs=[whole_vmem] * len(parts),
        out_specs=tuple([whole_vmem] * len(parts)),
        scratch_shapes=scatter_scratch(parts, devices),
        compiler_params=params(number),
    )(*parts)


def shards(devices, tokens, w_qkv, w_out, w_in, w_down, gain_attn, gain_mlp, cotangent):
    rows, wide = tokens.shape
    own = w_qkv.shape[0]
    scale = HEAD_DIM ** (-0.5)
    width_here = w_qkv.shape[2]
    hidden_here = w_in.shape[2]
    gains = jnp.concatenate(
        [gain_attn[:, None], gain_mlp[:, None], jnp.zeros((own, 126), bf16)], axis=1
    )
    full_qkv, full_in, out_turned, down_turned, full_gains = (
        x.reshape(wide, -1)
        for x in all_gather(
            (w_qkv.reshape(own, -1), w_in.reshape(own, -1), w_out.T, w_down.T, gains), devices, 0
        )
    )
    gain_first = full_gains[:, 0].astype(f32)
    gain_second = full_gains[:, 1].astype(f32)
    cosine, sine = rope_tables(lax.axis_index("ctx") * rows, rows)
    inputs = tokens.astype(f32)
    normed = layer_norm(inputs, gain_first).astype(bf16)
    mixed_qkv = nn(normed, full_qkv).reshape(rows, 3, width_here)
    query_heads = rotate(split_heads(mixed_qkv[:, 0]), cosine, sine).astype(bf16)
    key_heads = rotate(split_heads(mixed_qkv[:, 1]), cosine, sine).astype(bf16)
    query_rows = query_heads.reshape(rows, width_here) * jnp.asarray(scale, bf16)
    key_rows = key_heads.reshape(rows, width_here)
    value_rows = mixed_qkv[:, 2].astype(bf16)
    keys_all, values_all, attended, log_total = forward_attention(
        query_rows, key_rows, value_rows, devices, 1
    )
    attended_low = attended.astype(bf16)
    branch = head_sum(nt(attended_low, out_turned), 2)
    middle = inputs + branch
    normed_mlp, second_pull = jax.vjp(layer_norm, middle, gain_second)
    normed_mlp = normed_mlp.astype(bf16)
    gate_up = nn(normed_mlp, full_in).reshape(rows, 2, hidden_here)

    def activate(first, second):
        return jax.nn.gelu(first, approximate=False) * second

    hidden_values, activate_pull = jax.vjp(activate, gate_up[:, 0], gate_up[:, 1])
    hidden = hidden_values.astype(bf16)
    grad_hidden = nn(cotangent, down_turned)
    grad_pair = jnp.concatenate(activate_pull(grad_hidden), axis=1).astype(bf16)
    grad_normed_mlp = head_sum(nt(grad_pair, full_in), 3)
    grad_middle_norm, grad_gain_mlp = second_pull(grad_normed_mlp)
    grad_middle = cotangent.astype(f32) + grad_middle_norm
    grad_attn = grad_middle.astype(bf16)
    grad_rows = nn(grad_attn, out_turned).astype(bf16)
    correction = jnp.sum(split_heads(grad_rows.astype(f32) * attended), axis=2)
    heads_here = width_here // HEAD_DIM
    stats = jnp.concatenate(
        [log_total, correction.T, jnp.zeros((8 - heads_here, rows), f32)], axis=0
    )

    def tn(a, b):
        return lax.dot_general(
            a, b, (((0,), (0,)), ((), ())), preferred_element_type=f32
        ).astype(bf16)

    def blocks(part):
        return part.reshape(devices, own, -1)

    def with_gain(part, gain):
        return jnp.concatenate(
            [part, gain[:, None].astype(bf16), jnp.zeros((wide, 127), bf16)], axis=1
        )

    early = (
        blocks(tn(normed_mlp, grad_pair)),
        blocks(tn(cotangent, hidden)),
        blocks(with_gain(tn(grad_attn, attended_low), grad_gain_mlp)),
    )
    half = HEAD_DIM // 2
    grad_triple, branch_mlp, owned_in, owned_down, owned_out = backward_attention(
        query_rows, grad_rows, stats, key_rows, value_rows, keys_all, values_all,
        cosine[:, 0, :half].T, sine[:, 0, :half].T,
        nt(hidden, down_turned).astype(bf16), early, devices, 4,
    )
    mixed = (middle + branch_mlp).astype(bf16)
    grad_normed = head_sum(nt(grad_triple, full_qkv), 5)
    _, first_pull = jax.vjp(layer_norm, inputs, gain_first)
    grad_input_norm, grad_gain_attn = first_pull(grad_normed)
    grad_tokens = grad_middle + grad_input_norm

    cut = (3 * width_here // 2) // 128 * 128 + 128 * (3 * width_here % 256 > 0)
    owned_first, owned_second = reduce_scatter(
        (
            blocks(tn(normed, grad_triple[:, :cut])),
            blocks(with_gain(tn(normed, grad_triple[:, cut:]), grad_gain_attn)),
        ),
        devices,
        6,
    )
    rest = 3 * width_here - cut
    owned_qkv = jnp.concatenate([owned_first, owned_second[:, :rest]], axis=1)
    return (
        mixed,
        grad_tokens,
        owned_qkv.reshape(own, 3, width_here),
        owned_out[:, :width_here].T,
        owned_in.reshape(own, 2, hidden_here),
        owned_down.T,
        owned_second[:, rest],
        owned_out[:, width_here],
    )


def solution(mesh):
    in_specs = (
        P("ctx", None),
        P("ctx", None, "head"),
        P("head", "ctx"),
        P("ctx", None, "head"),
        P("head", "ctx"),
        P("ctx"),
        P("ctx"),
        P("ctx", None),
    )
    out_specs = (
        P("ctx", None),
        P("ctx", None),
        P("ctx", None, "head"),
        P("head", "ctx"),
        P("ctx", None, "head"),
        P("head", "ctx"),
        P("ctx"),
        P("ctx"),
    )
    return jax.shard_map(
        functools.partial(shards, mesh.shape["ctx"]),
        mesh=mesh, in_specs=in_specs, out_specs=out_specs, check_vma=False,
    )
```

time: 316 us -> 280 us (0.89)
  Pallas kernels: 233 us -> 207 us
  local copies, waits for them, and re-layouts: 35.3 us -> 27.7 us
    pallas_call x3, Pallas kernels: 140 us -> 124 us  [the longest x1 65.5 us: backward_attention(): pl.pallas_call(functools.partial(backward_kernel, devices, heads, near, l...]
    concatenate x2, local copies, waits for them, and re-layouts: 9.6 us -> 0.11 us  [the longest x1 0.08 us: shards(): jnp.concatenate([gain_attn[:, None], gain_mlp[:, None], jnp.zeros((own, 1...]
    pallas_call x3, Pallas kernels: 45.9 us -> 36.8 us  [head_sum(): pl.pallas_call(exchange_kernel, out_shape=jax.ShapeDtypeStruct(part.shape...]
    dot_general x0 -> x2, local copies, waits for them, and re-layouts: none -> 5.53 us  [nn(): return jnp.dot(a, b, preferred_element_type=f32)]
    dot_general x4, matrix products: 8.26 us -> 4.29 us  [nn(): return jnp.dot(a, b, preferred_element_type=f32)]
    mul x2 -> x0, local copies, waits for them, and re-layouts: 3.84 us -> none  [unrotate(): return values * cosine - turn_half(values) * sine]
where the time goes in v2:
time: 280 us; the launch traced here: 279 us
  Pallas kernels  207 us (74%)
  local copies, waits for them, and re-layouts  27.7 us (10%)
  other arithmetic  22.5 us (8%)
  matrix products  20.1 us (7%)
    pallas_call x1, Pallas kernels, backward_attention(): pl.pallas_call(functools.partial(backward_kernel, devices, heads, near, l...  65.5 us
    pallas_call x1, Pallas kernels, forward_attention(): pl.pallas_call(functools.partial(forward_kernel, devices, heads), out_sha...  46.3 us
    pallas_call x1, Pallas kernels, all_gather(): pl.pallas_call(functools.partial(gather_kernel, devices, len(own)), out_s...  38.7 us
    pallas_call x3, Pallas kernels, head_sum(): pl.pallas_call(exchange_kernel, out_shape=jax.ShapeDtypeStruct(part.shape...  36.8 us
    pallas_call x1, Pallas kernels, reduce_scatter(): pl.pallas_call(functools.partial(scatter_kernel, devices, len(parts)), ou...  20 us
    dot_general x4, matrix products, nt(): lax.dot_general(a, b, (((1,), (1,)), ((), ())), preferred_element_type=f32)  9.87 us
    dot_general x5, matrix products, tn(): lax.dot_general(a, b, (((0,), (0,)), ((), ())), preferred_element_type=f32)  5.95 us

profile of v2, /device:TPU:0, one launch (start us, length us, event | category | flops | bytes accessed | tf_op | source)
XLA Modules:
  0.0 279.0 jit_solution(3475119461641033069)
XLA Ops:
  0.6 1.6 copy.46
  2.2 1.7 reshape.325.refs_1_
  3.9 0.8 copy.27
  4.6 0.8 copy.26
  5.5 0.7 maximum_maximum_fusion.1.refs_4_
  6.1 38.7 %shard_map.143 = (bf16[16,48,1152]{2,1,0:T(8,128)(2,1)}, bf16[16,48,1152]{2,1,0:T(8,128)(2,1)}, bf16[16,48,384]{2,1,0:T(8,128)(2,1)}, bf16[16,48,576]{2,1,0:T(8,128)(2,1)}, bf16[16,48,128]{2,1,0:T(8,128)(2,1)}) custom-call(bf16[48,1152]{1,0:T(8,128)(2,1)} %bitcast.193, bf16[48,1152]{1,0:T(8,128)(2,1)} %reshape.325.refs_1_, bf16[48,384]{1,0:T(8,128)(2,1)} %bitcast.198, ...), custom_call_target="tpu_custom_call" | custom-call | tf_op jit(solution)/shard_map/pallas_call | solution.py:337
  44.9 2.7 copy.29
  47.6 0.8 fusion.140
  48.7 0.2 fusion.9
  49.0 0.8 fusion.49
  50.3 0.7 fusion.96
  51.0 0.8 fusion.90
  51.9 0.9 mul.265
  53.0 0.7 fusion.85.q.refs_0_
  53.9 0.7 fusion.46.k.refs_3_
  54.6 0.7 fusion.86.v.refs_4_
  55.3 46.3 %shard_map.144 = (bf16[16,256,384]{2,1,0:T(8,128)(2,1)}, bf16[16,256,384]{2,1,0:T(8,128)(2,1)}, f32[256,384]{1,0:T(8,128)}, f32[8,256]{1,0:T(8,128)}) custom-call(bf16[256,384]{1,0:T(8,128)(2,1)} %fusion.85.q.refs_0_, bf16[256,384]{1,0:T(8,128)(2,1)} %fusion.46.k.refs_3_, bf16[256,384]{1,0:T(8,128)(2,1)} %fusion.86.v.refs_4_), custom_call_target="tpu_custom_call" | custom-call | tf_op jit(solution)/shard_map/pallas_call | solution.py:477
  101.7 2.1 convolution_convert_fusion.8.own
  103.8 12.9 %shard_map.145 = f32[256,768]{1,0:T(8,128)} custom-call(bf16[256,768]{1,0:T(8,128)(2,1)} %convolution_convert_fusion.8.own), custom_call_target="tpu_custom_call" | custom-call | tf_op jit(solution)/shard_map/pallas_call | solution.py:668
  116.7 1.3 fusion.138
  118.0 2.8 %copy.37 = bf16[1152,768]{1,0:T(8,128)(2,1)S(1)} copy(bf16[1152,768]{0,1:T(8,128)(2,1)} %bitcast.181) | data formatting | bytes 3538944 | tf_op jit(solution)/shard_map/dot_general | solution.py:352
  121.3 0.7 fusion.43
  122.3 0.3 copy-done.34
  122.6 1.6 fusion.23
  124.4 0.6 copy-done.12
  125.2 0.6 copy-done.16
  125.8 0.4 copy-done.15
  126.2 1.5 convolution_convert_fusion.7.own
  127.6 12.0 %shard_map.146 = f32[256,768]{1,0:T(8,128)} custom-call(bf16[256,768]{1,0:T(8,128)(2,1)} %convolution_convert_fusion.7.own), custom_call_target="tpu_custom_call" | custom-call | tf_op jit(solution)/shard_map/pallas_call | solution.py:668
  139.6 2.0 multiply_reduce_fusion
  141.7 0.3 fusion.136
  142.2 0.5 copy-done.6
  142.9 1.2 convert_multiply_fusion
  144.1 1.9 copy.38
  146.0 1.6 reduce_sum.106
  147.7 1.4 maximum_maximum_fusion.refs_2_
  149.1 1.7 fusion.95
  150.8 3.7 %convolution_convert_fusion.6.refs_9_ = bf16[256,768]{1,0:T(8,128)(2,1)} fusion(bf16[768,576]{1,0:T(8,128)(2,1)} %bitcast.202, f32[256,2,576]{0,2,1:T(8,128)S(1)} %copy-done.4), kind=kOutput, calls=%fused_computation.7 | convolution fusion | flops 236421120 | bytes 2457600 | tf_op jit(solution)/shard_map/dot_general | solution.py:348
  154.6 2.0 convolution_convert_fusion
  156.6 1.4 fusion
  158.0 2.3 copy.39
  160.3 0.3 convert_element_type.178
  160.7 0.4 convolution_convert_fusion.4
  161.2 1.0 pad_maximum_fusion.1.refs_12_
  162.2 65.5 %shard_map.147 = (bf16[256,1152]{1,0:T(8,128)(2,1)}, f32[256,768]{1,0:T(8,128)}, f32[48,1152]{1,0:T(8,128)}, f32[48,576]{1,0:T(8,128)}, f32[48,512]{1,0:T(8,128)}) custom-call(bf16[256,384]{1,0:T(8,128)(2,1)} %fusion.85.q.refs_0_, bf16[256,384]{1,0:T(8,128)(2,1)} %get-tuple-element.84.refs_1_, f32[16,256]{1,0:T(8,128)} %maximum_maximum_fusion.refs_2_, ...), custom_call_target="tpu_custom_call" | custom-call | tf_op jit(solution)/shard_map/pallas_call | solution.py:619
  227.7 2.1 add_convert_fusion
  229.8 2.5 convolution_convert_fusion.5.own
  232.3 12.0 %shard_map.148 = f32[256,768]{1,0:T(8,128)} custom-call(bf16[256,768]{1,0:T(8,128)(2,1)} %convolution_convert_fusion.5.own), custom_call_target="tpu_custom_call" | custom-call | tf_op jit(solution)/shard_map/pallas_call | solution.py:668
  244.3 1.5 fusion.10
  245.8 1.6 fusion.8
  247.4 1.3 add_add_fusion.2
  248.6 1.6 convolution_convert_fusion.1
  250.2 0.3 convert_element_type.179
  250.6 0.5 convolution_convert_fusion.3
  251.1 1.1 pad_maximum_fusion.refs_1_
  252.3 20.0 %shard_map.149 = (f32[48,640]{1,0:T(8,128)}, f32[48,640]{1,0:T(8,128)}) custom-call(bf16[16,48,640]{2,1,0:T(8,128)(2,1)} %bitcast.189, bf16[16,48,640]{2,1,0:T(8,128)(2,1)} %pad_maximum_fusion.refs_1_), custom_call_target="tpu_custom_call" | custom-call | tf_op jit(solution)/shard_map/pallas_call | solution.py:698
  272.3 0.9 slice.73
  273.2 0.9 pad_maximum_fusion.5
  274.1 0.7 copy.48
  274.8 0.6 slice_bitcast_fusion
  275.4 0.9 reshape.336
  276.3 1.4 slice_reduce_fusion.1
  277.7 0.6 slice_reduce_fusion
  278.3 0.6 copy.50
  (98 shorter events, 2.8 us)
Async XLA Ops:
  44.9 2.7 copy-start.18
  44.9 3.7 %copy-start = (bf16[256,768]{1,0:T(8,128)(2,1)S(1)}, bf16[256,768]{1,0:T(8,128)(2,1)}, u32[]{:S(2)}) copy-start(bf16[256,768]{1,0:T(8,128)(2,1)} %param.8) | copy-start | bytes 1179652
  48.9 0.9 copy-start.29
  49.0 0.8 copy-start.27
  53.7 47.9 %copy-start.10 = (bf16[16,48,384]{2,1,0:T(8,128)(2,1)S(1)}, bf16[16,48,384]{2,1,0:T(8,128)(2,1)}, u32[]{:S(2)}) copy-start(bf16[16,48,384]{2,1,0:T(8,128)(2,1)} %get-tuple-element.27) | copy-start | bytes 1769476
  118.0 2.9 %copy-start.19 = (bf16[768,1]{1,0:T(8,128)(2,1)S(1)}, bf16[768,1]{1,0:T(8,128)(2,1)}, u32[]{:S(2)}) copy-start(bf16[768,1]{1,0:T(8,128)(2,1)} %get-tuple-element.72) | copy-start | bytes 4612
  121.3 20.4 %copy-start.25 = (f32[256]{0:T(256)}, f32[256]{0:T(256)S(1)}, u32[]{:S(2)}) copy-start(f32[256]{0:T(256)S(1)} %fusion.98) | copy-start | bytes 3076
  121.3 1.0 copy-start.5
  121.3 1.3 copy-start.34
  122.0 2.2 copy-start.3
  124.2 0.8 copy-start.12
  124.2 0.9 copy-start.20
  124.3 1.9 copy-start.15
  125.1 0.7 copy-start.16
  139.6 2.1 copy-start.2
  141.7 1.0 copy-start.6
  141.7 1.2 copy-start.11
  142.1 2.0 copy-start.31
  142.9 1.2 copy-start.8
  142.9 7.9 %copy-start.4 = (f32[256,2,576]{0,2,1:T(8,128)S(1)}, f32[256,2,576]{0,2,1:T(8,128)}, u32[]{:S(2)}) copy-start(f32[256,2,576]{0,2,1:T(8,128)} %copy-done.3) | copy-start | bytes 3538948
  150.8 3.8 %copy-start.17 = (bf16[256,576]{0,1:T(8,128)(2,1)S(1)}, bf16[256,576]{0,1:T(8,128)(2,1)}, u32[]{:S(2)}) copy-start(bf16[256,576]{0,1:T(8,128)(2,1)} %copy-done.16) | copy-start | bytes 884740
  150.8 3.8 %copy-start.21 = (bf16[256,576]{0,1:T(8,128)(2,1)S(1)}, bf16[256,576]{0,1:T(8,128)(2,1)}, u32[]{:S(2)}) copy-start(bf16[256,576]{0,1:T(8,128)(2,1)} %copy-done.20) | copy-start | bytes 884740
  150.8 3.8 %copy-start.26 = (f32[256]{0:T(256)S(1)}, f32[256]{0:T(256)}, u32[]{:S(2)}) copy-start(f32[256]{0:T(256)} %copy-done.25) | copy-start | bytes 3076
  154.6 2.1 copy-start.13
  156.6 3.7 %copy-start.33 = (bf16[768]{0:T(1024)(128)(2,1)S(1)}, bf16[768]{0:T(1024)(128)(2,1)}, u32[]{:S(2)}) copy-start(bf16[768]{0:T(1024)(128)(2,1)} %get-tuple-element.56) | copy-start | bytes 4612
  158.0 2.7 copy-start.7
  158.0 2.7 copy-start.9
  227.7 2.1 copy-start.14
  232.3 13.5 %copy-start.30 = (f32[256]{0:T(256)S(1)}, f32[256]{0:T(256)}, u32[]{:S(2)}) copy-start(f32[256]{0:T(256)} %copy-done.29) | copy-start | bytes 3076
  232.3 13.5 %copy-start.28 = (f32[256]{0:T(256)S(1)}, f32[256]{0:T(256)}, u32[]{:S(2)}) copy-start(f32[256]{0:T(256)} %copy-done.27) | copy-start | bytes 3076
  232.3 15.1 %copy-start.32 = (f32[256]{0:T(256)S(1)}, f32[256]{0:T(256)}, u32[]{:S(2)}) copy-start(f32[256]{0:T(256)} %copy-done.31) | copy-start | bytes 3076
  244.3 3.1 %copy-start.1 = (f32[256,768]{1,0:T(8,128)S(1)}, f32[256,768]{1,0:T(8,128)}, u32[]{:S(2)}) copy-start(f32[256,768]{1,0:T(8,128)} %shard_map.148) | copy-start | bytes 2359300
  247.3 1.3 copy-start.35
  252.3 22.5 %copy-start.24 = (f32[48,512]{1,0:T(8,128)S(1)}, f32[48,512]{1,0:T(8,128)}, u32[]{:S(2)}) copy-start(f32[48,512]{1,0:T(8,128)} %get-tuple-element.37) | copy-start | bytes 294916
  252.3 23.2 %copy-start.22 = (f32[48,1152]{1,0:T(8,128)S(1)}, f32[48,1152]{1,0:T(8,128)}, u32[]{:S(2)}) copy-start(f32[48,1152]{1,0:T(8,128)} %get-tuple-element.38) | copy-start | bytes 663556
  252.3 26.1 %copy-start.23 = (f32[48,576]{1,0:T(8,128)S(1)}, f32[48,576]{1,0:T(8,128)}, u32[]{:S(2)}) copy-start(f32[48,576]{1,0:T(8,128)} %get-tuple-element.39) | copy-start | bytes 331780
